TPU v7x, 128 devices: a whole 4x4x4 slice. The times are simulated.
128 devices in a mesh: rep: 32 (over x, z, y_lo), fsdp: 4 (over y_hi, core).
Axes of the slice: x: 4, y: 4 (y_hi: 2, y_lo: 2; y = y_hi * 2 + y_lo), z: 4, core: 2. Of those that a mesh axis runs over, the one named last changes fastest.
Arguments:
- tokens: bfloat16 [8192, 2560], P('rep', 'fsdp'), may hold values from -6 to 6
- seq_len: int32 [128], replicated, may hold values from 1 to 253, as said below
- seq_owner: int32 [128], replicated, may hold values from 0 to 31, as said below
- gain_1: bfloat16 [2560], P('fsdp'), may hold values from 0.099609375 to 1.8984375
- gain_2: bfloat16 [2560], P('fsdp'), may hold values from 0.099609375 to 1.8984375
- w_xy: bfloat16 [2, 2560, 10, 256], P(None, None, None, 'fsdp'), may hold values from -0.125 to 0.125
- conv_w: bfloat16 [4, 10, 256], P(None, None, 'fsdp'), may hold values from -3 to 3
- conv_b: bfloat16 [10, 256], P(None, 'fsdp'), may hold values from -2 to 2
- gate_w: bfloat16 [2, 10, 256, 256], P(None, None, None, 'fsdp'), may hold values from -0.375 to 0.375
- gate_b: bfloat16 [2, 10, 256], P(None, None, 'fsdp'), may hold values from -3 to 3
- a_param: float32 [10, 256], P(None, 'fsdp'), may hold values from -9 to -4
- w_out: bfloat16 [10, 256, 2560], P(None, 'fsdp'), may hold values from -0.3125 to 0.3125
- w_in: bfloat16 [2, 2560, 7680], P(None, None, 'fsdp'), may hold values from -0.125 to 0.125
- w_down: bfloat16 [7680, 2560], P('fsdp'), may hold values from -0.125 to 0.125
- cotangent: bfloat16 [8192, 2560], P('rep', 'fsdp'), may hold values from -6 to 6
Outputs:
- block_out: bfloat16 [8192, 2560], P('rep', 'fsdp')
- d_tokens: float32 [8192, 2560], P('rep', 'fsdp')
- d_gain_1: float32 [2560], P('fsdp')
- d_gain_2: float32 [2560], P('fsdp')
- d_w_xy: float32 [2, 2560, 10, 256], P(None, 'rep', None, 'fsdp')
- d_conv_w: float32 [4, 10, 256], P(None, None, 'fsdp')
- d_conv_b: float32 [10, 256], P(None, 'fsdp')
- d_gate_w: float32 [2, 10, 256, 256], P(None, None, 'rep', 'fsdp')
- d_gate_b: float32 [2, 10, 256], P(None, None, 'fsdp')
- d_a_param: float32 [10, 256], P(None, 'fsdp')
- d_w_out: float32 [10, 256, 2560], P(None, 'fsdp', 'rep')
- d_w_in: float32 [2, 2560, 7680], P(None, 'rep', 'fsdp')
- d_w_down: float32 [7680, 2560], P('fsdp', 'rep')
Inputs may be any that keep to these rules, and one draw needn't show every extreme that they name: `seq_len`: the sequences owned by one index of rep have lengths that sum to at most 256; in every draw one index's sequences fill all its 256 rows, and its first sequence is 253 long. `seq_owner`: each index of rep owns exactly 4 sequences.
All inputs are finite; a program needn't handle non-finite values.
Results may differ from a plain program's by a relative error of at most 0.025.
Values may be sent and summed in bfloat16 or wider, within the bound.
A program may use at most 320 MiB of HBM per device.

v0:
```python
import jax
import jax.numpy as jnp
from jax import lax
from jax.sharding import PartitionSpec as P

EPSILON = 1e-06


def gather_turned(arrays, axis, dims):
    turned = [jnp.moveaxis(a, dim, 0) for a, dim in zip(arrays, dims)]
    widths = [t[0].size for t in turned]
    both = jnp.concatenate([t.reshape(-1, w) for t, w in zip(turned, widths)], axis=1)
    filled = lax.all_gather(both, axis, axis=0, tiled=True)
    pieces = jnp.split(filled, [sum(widths[:k]) for k in range(1, len(widths))], axis=1)
    return tuple(
        (
            jnp.moveaxis(b.reshape(-1, *t.shape[1:]), 0, dim)
            for b, t, dim in zip(pieces, turned, dims)
        )
    )


def from_everyone(value, axis):
    devices = lax.axis_size(axis)
    return lax.all_to_all(
        jnp.broadcast_to(value[None], (devices, *value.shape)), axis, 0, 0, tiled=True
    )


def in_order(pieces, dim):
    dims = list(pieces.shape[1:])
    dims[dim] *= pieces.shape[0]
    return jnp.moveaxis(pieces, 0, dim).reshape(dims)


def gather_directly(value, axis, dim):
    pieces = from_everyone(value, axis)
    return in_order(pieces, dim)


def padded_to(lines, devices):
    spare = -len(lines) % devices
    return jnp.pad(lines, [(0, spare)] + [(0, 0)] * (lines.ndim - 1))


def sum_in_two_steps(value, axis):
    lines = value.reshape(-1, *value.shape[1:][-1:])
    padded = padded_to(lines, lax.axis_size(axis))
    own = lax.psum_scatter(padded, axis, scatter_dimension=0, tiled=True)
    whole = lax.all_gather(own, axis, axis=0, tiled=True)
    return whole[: len(lines)].reshape(value.shape)


def in_blocks(value, dim, devices):
    dims = value.shape
    pieces = value.reshape(*dims[:dim], devices, dims[dim] // devices, *dims[dim + 1 :])
    return jnp.moveaxis(pieces, dim, 0)


def sum_at_owner(value, axis, dim):
    pieces = in_blocks(value, dim, lax.axis_size(axis))
    arrived = lax.all_to_all(pieces, axis, split_axis=0, concat_axis=0, tiled=True)
    return arrived.astype(jnp.float32).sum(axis=0)


def taken_together(value, axis):
    everything = from_everyone(value, axis)
    return jnp.sum(everything, axis=0)


def sum_packed(arrays, axis, dims):
    devices = lax.axis_size(axis)
    pieces = [in_blocks(a, dim, devices) for a, dim in zip(arrays, dims)]
    lines = jnp.concatenate([b.reshape(devices, -1) for b in pieces], axis=1)
    span = max(16, -(-lines.shape[1] // 1024) * 8)
    lines = jnp.pad(lines, ((0, 0), (0, span * 128 - lines.shape[1]))).reshape(-1, 128)
    line, at, outs = (lax.psum_scatter(lines, axis, tiled=True).reshape(-1), 0, [])
    for b in pieces:
        part = b[0]
        outs.append(line[at : at + part.size].reshape(part.shape))
        at += part.size
    return tuple(outs)


def in_one(arrays, axis):
    ends = [0]
    for a in arrays:
        ends.append(ends[-1] + a.size)
    running = taken_together(jnp.concatenate([a.ravel() for a in arrays]), axis)
    return tuple((running[b:e].reshape(a.shape) for a, b, e in zip(arrays, ends, ends[1:])))


def gelu_tanh(value):
    return jax.nn.gelu(value, approximate=True)


def combine(earlier, later):
    return (earlier[0] * later[0], later[0] * earlier[1] + later[1])


def shift_rows(values, steps):
    if steps == 0:
        return values
    filler = jnp.zeros((steps,) + values.shape[1:], values.dtype)
    return jnp.concatenate([filler, values[: values.shape[0] - steps]], axis=0)


def lift_rows(values, steps):
    if steps == 0:
        return values
    filler = jnp.zeros((steps,) + values.shape[1:], values.dtype)
    return jnp.concatenate([values[steps:], filler], axis=0)


def tap_mask(segment, steps):
    filler = jnp.full((steps,), -1, jnp.int32)
    before = jnp.concatenate([filler, segment[: segment.shape[0] - steps]], axis=0)
    return (before == segment).astype(jnp.float32)[:, None]


def layout_of(seq_len, seq_owner, group_pos, capacity):
    seq_index = jnp.arange(seq_len.shape[0], dtype=jnp.int32)
    same_group = seq_owner[:, None] == seq_owner[None, :]
    earlier = same_group & (seq_index[None, :] < seq_index[:, None])
    offset = jnp.sum(jnp.where(earlier, seq_len[None, :], 0), axis=1)
    owned_here = seq_owner == group_pos
    total = jnp.sum(jnp.where(owned_here, seq_len, 0))
    places = jnp.arange(capacity, dtype=jnp.int32)
    start = jnp.any(owned_here[:, None] & (offset[:, None] == places[None, :]), axis=0).astype(
        jnp.int32
    )
    valid = (places < total).astype(jnp.float32)
    return (start, valid)


def body(
    tokens,
    seq_len,
    seq_owner,
    gain_1,
    gain_2,
    w_xy,
    conv_w,
    conv_b,
    gate_w,
    gate_b,
    a_param,
    w_out,
    w_in,
    w_down,
    cotangent,
):
    group_pos = lax.axis_index("rep")
    fsdp_pos = lax.axis_index("fsdp")
    capacity = tokens.shape[0]
    width_own = tokens.shape[1]
    width = width_own * lax.axis_size("fsdp")
    heads = w_xy.shape[2]
    block_own = w_xy.shape[3]
    channels = heads * block_own
    tap_count = conv_w.shape[0]
    start, valid = layout_of(seq_len, seq_owner, group_pos, capacity)
    segment = jnp.cumsum(start)
    keep = (1 - start).astype(jnp.float32)[:, None]
    is_start = (start == 1)[:, None]
    live = valid[:, None]
    rows, gain_one, gain_two = gather_turned((tokens, gain_1, gain_2), "fsdp", (1, 0, 0))
    rows_f = rows.astype(jnp.float32)
    gain_one_f = gain_one.astype(jnp.float32)
    gain_two_f = gain_two.astype(jnp.float32)
    r_one = lax.rsqrt(jnp.mean(rows_f * rows_f, axis=-1, keepdims=True) + EPSILON)
    n_one = (rows_f * r_one * gain_one_f).astype(jnp.bfloat16)
    w_pair = w_xy.reshape(2, width, channels)
    proj = jnp.einsum("td,kdc->ktc", n_one, w_pair, preferred_element_type=jnp.float32)
    x_branch = proj[0]
    y_branch = proj[1]
    y_gelu = gelu_tanh(y_branch)
    taps_w = conv_w.astype(jnp.float32).reshape(tap_count, channels)
    masks = [tap_mask(segment, tap) for tap in range(tap_count)]
    conv_f = conv_b.astype(jnp.float32).reshape(channels)[None, :] + jnp.zeros_like(x_branch)
    for tap in range(tap_count):
        conv_f = conv_f + taps_w[tap][None, :] * shift_rows(x_branch, tap) * masks[tap]
    conv_low = conv_f.astype(jnp.bfloat16)
    conv_full = gather_directly(conv_low.reshape(capacity, heads, block_own), "fsdp", 2)
    pre = jnp.einsum("thb,khbm->kthm", conv_full, gate_w, preferred_element_type=jnp.float32)
    pre = pre + gate_b.astype(jnp.float32)[:, None]
    gate_x = jax.nn.sigmoid(pre[0].reshape(capacity, channels))
    gate_a = jax.nn.sigmoid(pre[1].reshape(capacity, channels))
    decay_raw = a_param.reshape(channels)
    soft_decay = jax.nn.softplus(decay_raw)[None, :]
    decay = jnp.exp(-8.0 * gate_a * soft_decay)
    spread = 1.0 - decay * decay
    mult = jnp.where(is_start, 1.0, jnp.sqrt(jnp.maximum(spread, 0.01)))
    conv_v = conv_low.astype(jnp.float32)
    inflow = mult * gate_x * conv_v
    coeffs = decay * keep
    states = lax.associative_scan(combine, (coeffs, inflow), axis=0)[1]
    mixed = (states * y_gelu).astype(jnp.bfloat16)
    w_out_flat = w_out.reshape(channels, width)
    rec = sum_in_two_steps(jnp.dot(mixed, w_out_flat, preferred_element_type=jnp.float32), "fsdp")
    h_one = rows_f + rec
    r_two = lax.rsqrt(jnp.mean(h_one * h_one, axis=-1, keepdims=True) + EPSILON)
    n_two = (h_one * r_two * gain_two_f).astype(jnp.bfloat16)
    gate_up = jnp.einsum("td,kdf->ktf", n_two, w_in, preferred_element_type=jnp.float32)
    act_gate = gelu_tanh(gate_up[0])
    hidden = (act_gate * gate_up[1]).astype(jnp.bfloat16)
    mlp = sum_at_owner(
        jnp.dot(hidden, w_down, preferred_element_type=jnp.float32).astype(jnp.bfloat16), "fsdp", 1
    )
    h_own = lax.dynamic_slice_in_dim(h_one, fsdp_pos * width_own, width_own, 1)
    block_out = (live * (h_own + mlp)).astype(jnp.bfloat16)
    grad_rows = gather_directly(cotangent, "fsdp", 1)
    d_top = grad_rows.astype(jnp.float32) * live
    d_top_low = d_top.astype(jnp.bfloat16)
    d_hidden = jnp.einsum("td,fd->tf", d_top_low, w_down, preferred_element_type=jnp.float32)
    d_w_down = jnp.einsum("tf,td->fd", hidden, d_top_low, preferred_element_type=jnp.float32)
    _, gelu_pull = jax.vjp(gelu_tanh, gate_up[0])
    d_gate = gelu_pull(d_hidden * gate_up[1])[0]
    d_up = d_hidden * act_gate
    d_gate_up = jnp.stack([d_gate, d_up]).astype(jnp.bfloat16)
    d_w_in = jnp.einsum("td,ktf->kdf", n_two, d_gate_up, preferred_element_type=jnp.float32)
    red_w_in, red_w_down = (
        lax.psum_scatter(
            d_w_in.astype(jnp.bfloat16), "rep", scatter_dimension=1, tiled=True
        ).astype(jnp.float32),
        lax.psum_scatter(
            d_w_down.astype(jnp.bfloat16), "rep", scatter_dimension=1, tiled=True
        ).astype(jnp.float32),
    )
    d_n_two = lax.psum(
        jnp.einsum("ktf,kdf->td", d_gate_up, w_in, preferred_element_type=jnp.float32), "fsdp"
    )
    d_gain_two_all = jnp.sum(d_n_two * h_one * r_two, axis=0)
    v_two = d_n_two * gain_two_f
    d_h_one = (
        d_top + r_two * v_two - h_one * r_two**3 * jnp.mean(v_two * h_one, axis=-1, keepdims=True)
    )
    d_rec = d_h_one.astype(jnp.bfloat16)
    d_w_out = jnp.einsum("tc,td->cd", mixed, d_rec, preferred_element_type=jnp.float32)
    d_mixed = jnp.einsum("td,cd->tc", d_rec, w_out_flat, preferred_element_type=jnp.float32)
    d_states = d_mixed * y_gelu
    _, ygelu_pull = jax.vjp(gelu_tanh, y_branch)
    d_y_branch = ygelu_pull(d_mixed * states)[0]
    coeff_next = lift_rows(coeffs, 1)
    flipped = lax.associative_scan(
        combine, (jnp.flip(coeff_next, 0), jnp.flip(d_states, 0)), axis=0
    )[1]
    d_inflow = jnp.flip(flipped, 0)
    states_prev = shift_rows(states, 1)
    mult_slope = jnp.where(is_start | (spread <= 0.01), 0.0, -decay / mult)
    d_decay = d_inflow * states_prev * keep + d_inflow * gate_x * conv_v * mult_slope
    d_gate_x = d_inflow * mult * conv_v
    d_conv = d_inflow * mult * gate_x
    d_log = d_decay * decay
    d_decay_param = jnp.sum(d_log * (-8.0 * gate_a), axis=0) * jax.nn.sigmoid(decay_raw)
    d_pre_x = d_gate_x * gate_x * (1.0 - gate_x)
    d_pre_a = -8.0 * d_log * soft_decay * gate_a * (1.0 - gate_a)
    d_pre = (
        jnp.stack([d_pre_x, d_pre_a]).reshape(2, capacity, heads, block_own).astype(jnp.bfloat16)
    )
    d_gate_b = jnp.sum(d_pre.astype(jnp.float32), axis=1)
    d_gate_w = jnp.einsum("thb,kthm->khbm", conv_full, d_pre, preferred_element_type=jnp.float32)
    d_blocks = jnp.einsum("kthm,khbm->thb", d_pre, gate_w, preferred_element_type=jnp.float32)
    d_conv = d_conv + sum_at_owner(d_blocks.astype(jnp.bfloat16), "fsdp", 2).reshape(
        capacity, channels
    )
    d_conv_b = jnp.sum(d_conv, axis=0)
    d_conv_taps = []
    d_x_branch = jnp.zeros_like(x_branch)
    for tap in range(tap_count):
        masked = d_conv * masks[tap]
        d_conv_taps.append(jnp.sum(masked * shift_rows(x_branch, tap), axis=0))
        d_x_branch = d_x_branch + taps_w[tap][None, :] * lift_rows(masked, tap)
    d_conv_w = jnp.stack(d_conv_taps)
    d_pair = jnp.stack([d_x_branch, d_y_branch]).astype(jnp.bfloat16)
    d_w_xy = jnp.einsum("td,ktc->kdc", n_one, d_pair, preferred_element_type=jnp.float32)
    d_n_one_part = jnp.einsum("ktc,kdc->td", d_pair, w_pair, preferred_element_type=jnp.float32)
    gain_one_own = lax.dynamic_slice_in_dim(gain_one_f, fsdp_pos * width_own, width_own, 0)
    rows_own = lax.dynamic_slice_in_dim(rows_f, fsdp_pos * width_own, width_own, 1)
    d_h_own = lax.dynamic_slice_in_dim(d_h_one, fsdp_pos * width_own, width_own, 1)
    d_n_one = sum_at_owner(d_n_one_part.astype(jnp.bfloat16), "fsdp", 1)
    v_one = d_n_one * gain_one_own
    row_stat = taken_together(jnp.sum(v_one * rows_own, axis=-1, keepdims=True), "fsdp")
    d_tokens = d_h_own + r_one * v_one - rows_own * r_one**3 * row_stat / width
    d_gain_one = jnp.sum(d_n_one * rows_own * r_one, axis=0)
    d_gain_two = lax.dynamic_slice_in_dim(d_gain_two_all, fsdp_pos * width_own, width_own, 0)
    d_w_xy_four = d_w_xy.reshape(2, width, heads, block_own)
    d_w_out_three = d_w_out.reshape(heads, block_own, width)
    red_w_xy, red_gate_w, red_w_out = tuple(
        (
            part.astype(jnp.float32)
            for part in sum_packed(
                (
                    d_w_xy_four.astype(jnp.bfloat16),
                    d_gate_w.astype(jnp.bfloat16),
                    d_w_out_three.astype(jnp.bfloat16),
                ),
                "rep",
                (1, 2, 2),
            )
        )
    )
    sum_g1, sum_g2, sum_conv_w, sum_conv_b, sum_gate_b, sum_decay = in_one(
        (
            d_gain_one,
            d_gain_two,
            d_conv_w.reshape(tap_count, heads, block_own),
            d_conv_b.reshape(heads, block_own),
            d_gate_b,
            d_decay_param.reshape(heads, block_own),
        ),
        "rep",
    )
    return (
        block_out,
        d_tokens,
        sum_g1,
        sum_g2,
        red_w_xy,
        sum_conv_w,
        sum_conv_b,
        red_gate_w,
        sum_gate_b,
        sum_decay,
        red_w_out,
        red_w_in,
        red_w_down,
    )


def solution(mesh):
    return jax.shard_map(
        body,
        mesh=mesh,
        in_specs=(
            P("rep", "fsdp"),
            P(),
            P(),
            P("fsdp"),
            P("fsdp"),
            P(None, None, None, "fsdp"),
            P(None, None, "fsdp"),
            P(None, "fsdp"),
            P(None, None, None, "fsdp"),
            P(None, None, "fsdp"),
            P(None, "fsdp"),
            P(None, "fsdp", None),
            P(None, None, "fsdp"),
            P("fsdp", None),
            P("rep", "fsdp"),
        ),
        out_specs=(
            P("rep", "fsdp"),
            P("rep", "fsdp"),
            P("fsdp"),
            P("fsdp"),
            P(None, "rep", None, "fsdp"),
            P(None, None, "fsdp"),
            P(None, "fsdp"),
            P(None, None, "rep", "fsdp"),
            P(None, None, "fsdp"),
            P(None, "fsdp"),
            P(None, "fsdp", "rep"),
            P(None, "rep", "fsdp"),
            P("fsdp", "rep"),
        ),
        check_vma=False,
    )
```

profile of v0, /device:TPU:0, one launch (start us, length us, event | category | flops | bytes accessed | tf_op | source)
XLA Modules:
  0.0 1727.0 jit_solution(17847989584822011247)
XLA Ops:
  15.5 20.2 %all-gather.3.cloned.1.call-done = bf16[2560,258]{0,1:T(8,128)(2,1)} async-done(((bf16[640,258]{0,1:T(8,128)(2,1)}), bf16[2560,258]{0,1:T(8,128)(2,1)}) %all-gather.3.cloned.1.call-update) | async-done | bytes 1320976 | tf_op jit(solution)/shard_map/all_gather | solution.py:13
  55.7 18.7 %all-to-all-done = bf16[4,256,10,64]{1,3,2,0:T(8,128)(2,1)} async-done(((bf16[4,256,10,64]{1,3,2,0:T(8,128)(2,1)}), bf16[4,256,10,64]{1,3,2,0:T(8,128)(2,1)}, u32[]{:S(2)}, u32[]{:S(2)}) %all-to-all-start) | async-done | bytes 1310752 | tf_op jit(solution)/shard_map/all_to_all | solution.py:25
  166.9 40.6 %reduce-scatter.4.cloned.1.call-done = f32[64,2560]{1,0:T(8,128)} async-done(((f32[256,2560]{1,0:T(8,128)}), f32[64,2560]{1,0:T(8,128)}) %reduce-scatter.4.cloned.1.call-update) | async-done | bytes 655376 | tf_op jit(solution)/shard_map/reduce_scatter | solution.py:49
  214.8 28.4 %all-to-all-done.2 = bf16[4,256,640]{2,1,0:T(8,128)(2,1)} async-done(((bf16[4,256,640]{2,1,0:T(8,128)(2,1)}), bf16[4,256,640]{2,1,0:T(8,128)(2,1)}, u32[]{:S(2)}, u32[]{:S(2)}) %all-to-all-start.2) | async-done | bytes 1310752 | tf_op jit(solution)/shard_map/all_to_all | solution.py:25
  255.9 9.9 convolution_bitcast_fusion.2
  265.9 9.1 fusion.36
  276.3 11.0 convolution_bitcast_fusion.1
  287.7 11.6 convert_bitcast_fusion
  299.3 48.7 %copy.222 = bf16[2,2560,1920]{2,0,1:T(2,128)(2,1)} copy(bf16[2,2560,1920]{1,2,0:T(8,128)(2,1)} %convert_bitcast_fusion) | data formatting | bytes 39321600 | tf_op jit(solution)/shard_map/convert_element_type | solution.py:224
  407.7 7.9 convolution_convert_fusion
  428.3 7.4 convert_element_type.254
  442.6 12.6 reshape.342
  469.8 17.7 %convert_element_type.250 = bf16[2,32,80,10,64]{2,1,4,3,0:T(8,128)(2,1)} reshape(bf16[2,2560,640]{1,2,0:T(8,128)(2,1)} %convert_bitcast_fusion.1) | data formatting | bytes 13107200 | tf_op jit(solution)/shard_map/convert_element_type | solution.py:294
  487.4 23.7 %copy.216 = bf16[2,32,80,10,64]{4,3,2,0,1:T(8,128)(2,1)} copy(bf16[2,32,80,10,64]{2,1,4,3,0:T(8,128)(2,1)} %convert_element_type.250) | data formatting | bytes 13107200 | tf_op jit(solution)/shard_map/convert_element_type | solution.py:294
  511.1 27.0 %reshape.339 = bf16[32,102400]{1,0:T(8,128)(2,1)} reshape(bf16[32,2,80,10,64]{4,3,2,1,0:T(8,128)(2,1)} %bitcast.218) | data formatting | bytes 13107200 | tf_op jit(solution)/shard_map/reshape | solution.py:74
  538.1 10.7 pad_maximum_fusion
  548.8 10.6 reshape.343
  572.0 8.1 convolution_convert_fusion.2
  581.6 38.1 %all-to-all-done.4 = bf16[4,256,640]{2,1,0:T(8,128)(2,1)S(1)} async-done(((bf16[4,256,640]{2,1,0:T(8,128)(2,1)}), bf16[4,256,640]{2,1,0:T(8,128)(2,1)S(1)}, u32[]{:S(2)}, u32[]{:S(2)}) %all-to-all-start.4) | async-done | bytes 1310752 | tf_op jit(solution)/shard_map/all_to_all | solution.py:62
  627.3 46.4 %all-to-all-done.1 = bf16[4,256,640]{2,1,0:T(8,128)(2,1)} async-done(((bf16[4,256,640]{2,1,0:T(8,128)(2,1)}), bf16[4,256,640]{2,1,0:T(8,128)(2,1)}, u32[]{:S(2)}, u32[]{:S(2)}) %all-to-all-start.1) | async-done | bytes 1310752 | tf_op jit(solution)/shard_map/all_to_all | solution.py:62
  698.8 10.0 all-to-all-done.6
  713.8 537.2 %all-reduce.48.cloned.1.call-done = bf16[2,2560,1920]{2,0,1:T(2,128)(2,1)} async-done(((bf16[2,2560,1920]{2,0,1:T(2,128)(2,1)}), bf16[2,2560,1920]{2,0,1:T(2,128)(2,1)}) %all-reduce.48.cloned.1.call-update) | async-done | bytes 19660816
  1253.5 222.6 %reduce-scatter.8.cloned.1.call-done = bf16[1920,80]{0,1:T(8,128)(2,1)} async-done(((bf16[1920,2560]{0,1:T(8,128)(2,1)}), bf16[1920,80]{0,1:T(8,128)(2,1)}) %reduce-scatter.8.cloned.1.call-update) | async-done | bytes 307216 | tf_op jit(solution)/shard_map/reduce_scatter | solution.py:226
  1477.9 231.8 %reduce-scatter.6.cloned.1.call-done = bf16[1280,128]{1,0:T(8,128)(2,1)} async-done(((bf16[40960,128]{1,0:T(8,128)(2,1)}), bf16[1280,128]{1,0:T(8,128)(2,1)}) %reduce-scatter.6.cloned.1.call-update) | async-done | bytes 327696 | tf_op jit(solution)/shard_map/reduce_scatter | solution.py:77
  (502 shorter events, 300.2 us)
Async XLA Ops:
  7.2 156.2 %copy-start = (bf16[10,64,2560]{2,1,0:T(8,128)(2,1)S(1)}, bf16[10,64,2560]{2,1,0:T(8,128)(2,1)}, u32[]{:S(2)}) copy-start(bf16[10,64,2560]{2,1,0:T(8,128)(2,1)} %param.26) | copy-start | bytes 9830404
  7.2 28.5 %all-gather.3.cloned.1.call-start = ((), (), s32[]{:S(2)}) async-start(), calls=%async_computation.10 | async-start | bytes 1689600 | tf_op jit(solution)/shard_map/all_gather | solution.py:13
  13.0 69.1 %copy-start.71 = (pred[256]{0:T(512)(128)(4,1)}, pred[256]{0:T(512)(128)(4,1)S(1)}, u32[]{:S(2)}) copy-start(pred[256]{0:T(512)(128)(4,1)S(1)} %get-tuple-element.174) | copy-start | bytes 772
  15.1 29.3 %copy-start.52 = (f32[640]{0:T(1024)}, f32[640]{0:T(1024)S(1)}, u32[]{:S(2)}) copy-start(f32[640]{0:T(1024)S(1)} %mul.636) | copy-start | bytes 7684
  15.2 29.2 %copy-start.54 = (f32[640]{0:T(1024)}, f32[640]{0:T(1024)S(1)}, u32[]{:S(2)}) copy-start(f32[640]{0:T(1024)S(1)} %mul.631) | copy-start | bytes 7684
  15.2 29.1 %copy-start.56 = (f32[640]{0:T(1024)}, f32[640]{0:T(1024)S(1)}, u32[]{:S(2)}) copy-start(f32[640]{0:T(1024)S(1)} %mul.626) | copy-start | bytes 7684
  15.5 28.9 %copy-start.65 = (f32[256]{0:T(256)}, f32[256]{0:T(256)S(1)}, u32[]{:S(2)}) copy-start(f32[256]{0:T(256)S(1)} %get-tuple-element.171) | copy-start | bytes 3076
  15.5 28.9 %copy-start.67 = (f32[256]{0:T(256)}, f32[256]{0:T(256)S(1)}, u32[]{:S(2)}) copy-start(f32[256]{0:T(256)S(1)} %get-tuple-element.172) | copy-start | bytes 3076
  15.5 28.9 %copy-start.69 = (f32[256]{0:T(256)}, f32[256]{0:T(256)S(1)}, u32[]{:S(2)}) copy-start(f32[256]{0:T(256)S(1)} %get-tuple-element.173) | copy-start | bytes 3076
  51.2 23.2 %all-to-all-start = ((bf16[4,256,10,64]{1,3,2,0:T(8,128)(2,1)}), bf16[4,256,10,64]{1,3,2,0:T(8,128)(2,1)}, u32[]{:S(2)}, u32[]{:S(2)}) async-start(bf16[4,256,10,64]{1,3,2,0:T(8,128)(2,1)} %broadcast_in_dim.51), calls=%async_computation | async-start | bytes 2621440 | tf_op jit(solution)/shard_map/all_to_all | solution.py:25
  55.5 151.9 %reduce-scatter.4.cloned.1.call-start = ((), (), s32[]{:S(2)}) async-start(), calls=%async_computation.11 | async-start | bytes 3276800 | tf_op jit(solution)/shard_map/reduce_scatter | solution.py:49
  166.8 85.0 %all-gather.5.cloned.1.call-start = ((), (), s32[]{:S(2)}) async-start(), calls=%async_computation.12 | async-start | bytes 3276800 | tf_op jit(solution)/shard_map/all_gather | solution.py:50
  209.6 33.5 %all-to-all-start.2 = ((bf16[4,256,640]{2,1,0:T(8,128)(2,1)}), bf16[4,256,640]{2,1,0:T(8,128)(2,1)}, u32[]{:S(2)}, u32[]{:S(2)}) async-start(bf16[4,256,640]{2,1,0:T(8,128)(2,1)} %broadcast_in_dim.52), calls=%async_computation.3 | async-start | bytes 2621440 | tf_op jit(solution)/shard_map/all_to_all | solution.py:25
  213.9 157.6 %all-reduce.46.cloned.1.call-start = ((), (), s32[]{:S(2)}) async-start(), calls=%async_computation.13 | async-start | bytes 5242880 | tf_op jit(solution)/shard_map/psum | solution.py:230
  287.3 963.7 %all-reduce.48.cloned.1.call-start = ((), (), s32[]{:S(2)}) async-start(), calls=%async_computation.16 | async-start | bytes 39321600
  403.2 53.4 %all-to-all-start.3 = ((bf16[4,256,10,64]{1,3,2,0:T(8,128)(2,1)}), bf16[4,256,10,64]{1,3,2,0:T(8,128)(2,1)}, u32[]{:S(2)}, u32[]{:S(2)}) async-start(bf16[4,256,10,64]{1,3,2,0:T(8,128)(2,1)} %bitcast.212), calls=%async_computation.4 | async-start | bytes 2621440 | tf_op jit(solution)/shard_map/all_to_all | solution.py:62
  407.6 1068.5 %reduce-scatter.8.cloned.1.call-start = ((), (), s32[]{:S(2)}) async-start(), calls=%async_computation.15 | async-start | bytes 10137600 | tf_op jit(solution)/shard_map/reduce_scatter | solution.py:226
  415.7 1294.1 %reduce-scatter.6.cloned.1.call-start = ((), (), s32[]{:S(2)}) async-start(), calls=%async_computation.14 | async-start | bytes 10813440 | tf_op jit(solution)/shard_map/reduce_scatter | solution.py:77
  568.4 51.3 %all-to-all-start.4 = ((bf16[4,256,640]{2,1,0:T(8,128)(2,1)}), bf16[4,256,640]{2,1,0:T(8,128)(2,1)S(1)}, u32[]{:S(2)}, u32[]{:S(2)}) async-start(bf16[4,256,640]{2,1,0:T(8,128)(2,1)} %bitcast.231), calls=%async_computation.5 | async-start | bytes 2621440 | tf_op jit(solution)/shard_map/all_to_all | solution.py:62
  620.7 53.0 %all-to-all-start.1 = ((bf16[4,256,640]{2,1,0:T(8,128)(2,1)}), bf16[4,256,640]{2,1,0:T(8,128)(2,1)}, u32[]{:S(2)}, u32[]{:S(2)}) async-start(bf16[4,256,640]{2,1,0:T(8,128)(2,1)} %bitcast.230), calls=%async_computation.2 | async-start | bytes 2621440 | tf_op jit(solution)/shard_map/all_to_all | solution.py:62
  625.3 52.5 %copy-start.59 = (f32[640]{0:T(1024)S(1)}, f32[640]{0:T(1024)}, u32[]{:S(2)}) copy-start(f32[640]{0:T(1024)} %copy-done.58) | copy-start | bytes 7684
  626.9 64.9 %copy-start.78 = (u32[128]{0:T(128)S(1)}, u32[128]{0:T(128)}, u32[]{:S(2)}) copy-start(u32[128]{0:T(128)} %constant.156) | copy-start | bytes 1540
  674.3 9.0 all-to-all-start.5
  684.6 24.2 %all-to-all-start.6 = ((f32[32,1,6400]{2,1,0:T(1,128)}), f32[32,1,6400]{2,1,0:T(1,128)}, u32[]{:S(2)}, u32[]{:S(2)}) async-start(f32[32,1,6400]{2,1,0:T(1,128)} %broadcast_in_dim.55), calls=%async_computation.7 | async-start | bytes 1638400 | tf_op jit(solution)/shard_map/all_to_all | solution.py:25
  (71 other events, 294.0 us)
Sparse Core Ops, SparseCore 0:
  10.8 24.9 all-gather.2
  167.0 40.4 reduce-scatter.3
  209.2 38.9 all-gather.4
  287.4 66.2 all-reduce.45
  356.2 894.6 all-reduce.47
  1253.4 222.7 reduce-scatter.7
  1478.5 231.2 reduce-scatter.5
where the time goes:
time: 1740 us; the launch traced here: 1730 us
  waiting for transfers between devices  1200 us (69%)
  local copies, waits for them, and re-layouts  302 us (17%)
  other arithmetic  92.3 us (5%)
  matrix products  82.6 us (5%)
  starting transfers between devices  32.7 us (2%)
    unnamed x8, waiting for transfers between devices  537 us
    reduce_scatter x1, waiting for transfers between devices, sum_packed(): lax.psum_scatter(lines, axis, tiled=True).reshape(-1)  232 us
    reduce_scatter x1, waiting for transfers between devices, body(): lax.psum_scatter(d_w_down.astype(jnp.bfloat16), 'rep', scatter_dimension=...  223 us
    all_to_all x3, waiting for transfers between devices, sum_at_owner(): lax.all_to_all(pieces, axis, split_axis=0, concat_axis=0, tiled=True)  85.8 us
    all_to_all x4, waiting for transfers between devices, from_everyone(): lax.all_to_all(jnp.broadcast_to(value[None], (devices, *value.shape)), ax...  62.5 us
    convert_element_type x1, local copies, waits for them, and re-layouts, body(): d_w_in.astype(jnp.bfloat16)  48.7 us
    reshape x3, local copies, waits for them, and re-layouts, sum_packed(): lines = jnp.concatenate([b.reshape(devices, -1) for b in pieces], axis=1)  42.5 us
    slice x46, local copies, waits for them, and re-layouts, body(): states = lax.associative_scan(combine, (coeffs, inflow), axis=0)[1]  42.5 us
  transfers between devices with their start and end apart: 14, of which 12 were waited for; matrix products, arithmetic and copies ran while one was open for 18% of the time, Pallas kernels for 0%

commit v1 on v0

--- a/solution.py
+++ b/solution.py
@@ -1,9 +1,218 @@
+import functools
+
 import jax
 import jax.numpy as jnp
 from jax import lax
+from jax.experimental import pallas as pl
+from jax.experimental.pallas import tpu as pltpu
 from jax.sharding import PartitionSpec as P
 
 EPSILON = 1e-06
+
+MESH = pl.DeviceIdType.MESH
+VM = 60 * 2**20
+GC = 0.7978845608028654
+
+def gelu_parts(v):
+    v2 = v * v
+    t = jnp.tanh(GC * v * (1.0 + 0.044715 * v2))
+    half = 0.5 * (1.0 + t)
+    g = v * half
+    dg = half + 0.5 * v * (1.0 - t * t) * (GC * (1.0 + 3 * 0.044715 * v2))
+    return g, dg
+
+def dot(a, b):
+    return jnp.dot(a, b, preferred_element_type=jnp.float32)
+
+def dot_nt(a, b):
+    return lax.dot_general(a, b, (((1,), (1,)), ((), ())), preferred_element_type=jnp.float32)
+
+def ffn_kernel(n2, dt, w_in, w_dn, hid, dg, du, mlp, dn2, am, ad):
+    i = pl.program_id(0)
+    @pl.when(i == 0)
+    def _():
+        am[...] = jnp.zeros_like(am)
+        ad[...] = jnp.zeros_like(ad)
+    gate = dot(n2[...], w_in[0])
+    up = dot(n2[...], w_in[1])
+    g, dgl = gelu_parts(gate)
+    h = (g * up).astype(jnp.bfloat16)
+    hid[0] = h
+    dh = dot_nt(dt[...], w_dn[...])
+    a = (dh * up * dgl).astype(jnp.bfloat16)
+    b = (dh * g).astype(jnp.bfloat16)
+    dg[0] = a
+    du[0] = b
+    am[...] += dot(h, w_dn[...])
+    ad[...] += dot_nt(a, w_in[0])
+    ad[...] += dot_nt(b, w_in[1])
+    @pl.when(i == 2)
+    def _():
+        mlp[...] = am[...].astype(jnp.bfloat16)
+        dn2[...] = ad[...].astype(jnp.bfloat16)
+
+def ffn(n2, dt, w_in, w_dn):
+    R, D = n2.shape
+    T = 640
+    nt = w_dn.shape[0] // T
+    full = pl.BlockSpec((R, D), lambda i: (0, 0))
+    tile = pl.BlockSpec((1, R, T), lambda i: (i, 0, 0))
+    ch = jax.ShapeDtypeStruct((nt, R, T), jnp.bfloat16)
+    rd = jax.ShapeDtypeStruct((R, D), jnp.bfloat16)
+    return pl.pallas_call(
+        ffn_kernel, grid=(nt,),
+        in_specs=[full, full, pl.BlockSpec((2, D, T), lambda i: (0, 0, i)), pl.BlockSpec((T, D), lambda i: (i, 0))],
+        out_specs=[tile, tile, tile, full, full],
+        out_shape=[ch, ch, ch, rd, rd],
+        scratch_shapes=[pltpu.VMEM((R, D), jnp.float32)] * 2,
+        compiler_params=pltpu.CompilerParams(vmem_limit_bytes=VM),
+        name="ffn",
+    )(n2, dt, w_in, w_dn)
+
+def coords():
+    r = lax.axis_index("rep")
+    f = lax.axis_index("fsdp")
+    return r // 8, (r // 2) % 4, r % 2, f
+
+def peer(axis, d):
+    x, z, y, f = coords()
+    if axis == "x":
+        x = (x + d) % 4
+    elif axis == "z":
+        z = (z + d) % 4
+    elif axis == "y":
+        y = 1 - y
+    else:
+        f = f ^ d
+    return ((x * 4 + z) * 2 + y, f)
+
+class Grads:
+    def __init__(self, plan, fplan):
+        self.plan = plan
+        self.fplan = fplan
+    def scratch(self):
+        n, m = len(self.plan), len(self.fplan)
+        b = jnp.bfloat16
+        return [
+            pltpu.VMEM((n, 4, 256, 640), b),
+            pltpu.VMEM((m, 4, 160, 1024), b),
+            pltpu.VMEM((n, 4, 160, 640), b),
+            pltpu.VMEM((n, 3, 160, 640), b),
+            pltpu.VMEM((n, 2, 80, 640), b),
+            pltpu.VMEM((n, 80, 640), b),
+            pltpu.SemaphoreType.DMA((n, 3)), pltpu.SemaphoreType.DMA((n, 3)),
+            pltpu.SemaphoreType.DMA((m, 3)), pltpu.SemaphoreType.DMA((m, 3)),
+            pltpu.SemaphoreType.DMA((n, 3)), pltpu.SemaphoreType.DMA((n, 3)),
+            pltpu.SemaphoreType.DMA((n,)), pltpu.SemaphoreType.DMA((n,)),
+            pltpu.SemaphoreType.DMA((n,)), pltpu.SemaphoreType.DMA((m,)),
+        ]
+    def bind(self, refs, usrc, fsrc, out):
+        (self.ub, self.ft, self.st, self.rr, self.tt, self.yr, self.us, self.ur, self.fs, self.fr,
+         self.rq, self.rv, self.ys, self.yv, self.lu, self.lf) = refs
+        self.usrc, self.fsrc, self.out = usrc, fsrc, out
+    def rc(self, src, dst, s, r, axis, d):
+        return pltpu.make_async_remote_copy(src_ref=src, dst_ref=dst, send_sem=s, recv_sem=r, device_id=peer(axis, d), device_id_type=MESH)
+    def fcopies(self, k):
+        i, axis = self.fplan[k]
+        x, z, y, f = coords()
+        src = self.fsrc[i]
+        me = x if axis == "x" else z
+        pick = (lambda t: src.at[t]) if axis == "x" else (lambda t: src.at[:, t])
+        loc = pltpu.make_async_copy(pick(me), self.ft.at[k, :, :, pl.ds(0, 256)], self.lf.at[k])
+        rem = [self.rc(pick((me + d) % 4), self.ft.at[k, :, :, pl.ds(d * 256, 256)], self.fs.at[k, d - 1], self.fr.at[k, d - 1], axis, d) for d in (1, 3, 2)]
+        return loc, rem
+    def ucopies(self, c):
+        k, axis = self.plan[c]
+        src = self.usrc(c)
+        loc = pltpu.make_async_copy(src, self.ub.at[c, 0], self.lu.at[c])
+        rem = [self.rc(src, self.ub.at[c, d], self.us.at[c, d - 1], self.ur.at[c, d - 1], axis, d) for d in (1, 3, 2)]
+        return loc, rem
+    def rscopies(self, c):
+        k, axis = self.plan[c]
+        ra = "z" if axis == "x" else "x"
+        x, z, y, f = coords()
+        me = z if axis == "x" else x
+        return me, [self.rc(self.st.at[c, (me + d) % 4], self.rr.at[c, d - 1], self.rq.at[c, d - 1], self.rv.at[c, d - 1], ra, d) for d in (1, 3, 2)]
+    def ycopy(self, c):
+        x, z, y, f = coords()
+        return self.rc(self.tt.at[c, 1 - y], self.yr.at[c], self.ys.at[c], self.yv.at[c], "y", 0)
+    def send_f(self, k):
+        loc, rem = self.fcopies(k)
+        loc.start()
+        for r in rem: r.start()
+    def send_u(self, c):
+        loc, rem = self.ucopies(c)
+        loc.start()
+        for r in rem: r.start()
+    def mm(self, c):
+        k, axis = self.plan[c]
+        loc, rem = self.ucopies(c)
+        loc.wait()
+        for r in rem: r.wait()
+        if not self.fdone[k]:
+            loc, rem = self.fcopies(k)
+            loc.wait()
+            for r in rem: r.wait()
+            self.fdone[k] = True
+        self.st[c] = dot(self.ft[k].reshape(640, 1024), self.ub[c].reshape(1024, 640)).astype(jnp.bfloat16).reshape(4, 160, 640)
+        me, cps = self.rscopies(c)
+        for r in cps: r.start()
+    def rs(self, c):
+        me, cps = self.rscopies(c)
+        for r in cps: r.wait()
+        f = jnp.float32
+        t = (self.st[c, me].astype(f) + self.rr[c, 0].astype(f)) + (self.rr[c, 1].astype(f) + self.rr[c, 2].astype(f))
+        self.tt[c] = t.astype(jnp.bfloat16).reshape(2, 80, 640)
+        self.ycopy(c).start()
+    def fin(self, c):
+        x, z, y, f = coords()
+        self.ycopy(c).wait()
+        self.out[c] = self.tt[c, y].astype(jnp.float32) + self.yr[c].astype(jnp.float32)
+
+def entry_barrier(peers):
+    b = pltpu.get_barrier_semaphore()
+    for axis, d in peers:
+        pl.semaphore_signal(b, inc=1, device_id=peer(axis, d), device_id_type=MESH)
+    pl.semaphore_wait(b, len(peers))
+
+REP = [("x", 1), ("x", 2), ("x", 3), ("z", 1), ("z", 2), ("z", 3), ("y", 1)]
+
+PLAN = [(0, "x")] * 6 + [(1, "z")] * 3 + [(2, "x"), (3, "z"), (4, "z")]
+FPLAN = [(0, "x"), (1, "z"), (2, "x"), (2, "z"), (3, "z")]
+
+def grads_kernel(g, n2t, dtt, n1t, drt, dgs, dus, hids, dxs, zs, out, *refs):
+    def usrc(c):
+        if c < 3: return dgs.at[c]
+        if c < 6: return dus.at[c - 3]
+        if c < 9: return hids.at[c - 6]
+        if c < 11: return dxs.at[c - 9]
+        return zs
+    g.bind(refs, usrc, [n2t, dtt, n1t, drt], out)
+    g.fdone = [False] * len(g.fplan)
+    entry_barrier(REP)
+    g.send_f(0); g.send_f(1)
+    order = [0, 6, 1, 3, 7, 2, 4, 8, 5, 9, 10, 11]
+    for j, c in enumerate(order):
+        if j == 6:
+            for k in (2, 3, 4): g.send_f(k)
+        g.send_u(c)
+    n = len(order)
+    for j in range(n + 4):
+        if j < n: g.mm(order[j])
+        if 0 <= j - 2 < n: g.rs(order[j - 2])
+        if 0 <= j - 4 < n: g.fin(order[j - 4])
+
+def grads(n2t, dtt, n1t, drt, dgs, dus, hids, dxs, zs):
+    g = Grads(PLAN, FPLAN)
+    return pl.pallas_call(
+        functools.partial(grads_kernel, g),
+        out_shape=jax.ShapeDtypeStruct((12, 80, 640), jnp.float32),
+        in_specs=[pl.BlockSpec(memory_space=pl.ANY)] * 9,
+        out_specs=pl.BlockSpec(memory_space=pltpu.VMEM),
+        scratch_shapes=g.scratch(),
+        compiler_params=pltpu.CompilerParams(collective_id=7, has_side_effects=True, vmem_limit_bytes=VM),
+        name="grads",
+    )(n2t, dtt, n1t, drt, dgs, dus, hids, dxs, zs)
 
 
 def gather_turned(arrays, axis, dims):
@@ -201,42 +410,20 @@
     h_one = rows_f + rec
     r_two = lax.rsqrt(jnp.mean(h_one * h_one, axis=-1, keepdims=True) + EPSILON)
     n_two = (h_one * r_two * gain_two_f).astype(jnp.bfloat16)
-    gate_up = jnp.einsum("td,kdf->ktf", n_two, w_in, preferred_element_type=jnp.float32)
-    act_gate = gelu_tanh(gate_up[0])
-    hidden = (act_gate * gate_up[1]).astype(jnp.bfloat16)
-    mlp = sum_at_owner(
-        jnp.dot(hidden, w_down, preferred_element_type=jnp.float32).astype(jnp.bfloat16), "fsdp", 1
-    )
-    h_own = lax.dynamic_slice_in_dim(h_one, fsdp_pos * width_own, width_own, 1)
-    block_out = (live * (h_own + mlp)).astype(jnp.bfloat16)
     grad_rows = gather_directly(cotangent, "fsdp", 1)
     d_top = grad_rows.astype(jnp.float32) * live
     d_top_low = d_top.astype(jnp.bfloat16)
-    d_hidden = jnp.einsum("td,fd->tf", d_top_low, w_down, preferred_element_type=jnp.float32)
-    d_w_down = jnp.einsum("tf,td->fd", hidden, d_top_low, preferred_element_type=jnp.float32)
-    _, gelu_pull = jax.vjp(gelu_tanh, gate_up[0])
-    d_gate = gelu_pull(d_hidden * gate_up[1])[0]
-    d_up = d_hidden * act_gate
-    d_gate_up = jnp.stack([d_gate, d_up]).astype(jnp.bfloat16)
-    d_w_in = jnp.einsum("td,ktf->kdf", n_two, d_gate_up, preferred_element_type=jnp.float32)
-    red_w_in, red_w_down = (
-        lax.psum_scatter(
-            d_w_in.astype(jnp.bfloat16), "rep", scatter_dimension=1, tiled=True
-        ).astype(jnp.float32),
-        lax.psum_scatter(
-            d_w_down.astype(jnp.bfloat16), "rep", scatter_dimension=1, tiled=True
-        ).astype(jnp.float32),
-    )
-    d_n_two = lax.psum(
-        jnp.einsum("ktf,kdf->td", d_gate_up, w_in, preferred_element_type=jnp.float32), "fsdp"
-    )
+    hid_t, dg_t, du_t, mlp_low, dn2_low = ffn(n_two, d_top_low, w_in, w_down)
+    mlp = sum_at_owner(mlp_low, "fsdp", 1)
+    d_n_two = lax.psum(dn2_low.astype(jnp.float32), "fsdp")
+    h_own = lax.dynamic_slice_in_dim(h_one, fsdp_pos * width_own, width_own, 1)
+    block_out = (live * (h_own + mlp)).astype(jnp.bfloat16)
     d_gain_two_all = jnp.sum(d_n_two * h_one * r_two, axis=0)
     v_two = d_n_two * gain_two_f
     d_h_one = (
         d_top + r_two * v_two - h_one * r_two**3 * jnp.mean(v_two * h_one, axis=-1, keepdims=True)
     )
     d_rec = d_h_one.astype(jnp.bfloat16)
-    d_w_out = jnp.einsum("tc,td->cd", mixed, d_rec, preferred_element_type=jnp.float32)
     d_mixed = jnp.einsum("td,cd->tc", d_rec, w_out_flat, preferred_element_type=jnp.float32)
     d_states = d_mixed * y_gelu
     _, ygelu_pull = jax.vjp(gelu_tanh, y_branch)
@@ -273,7 +460,6 @@
         d_x_branch = d_x_branch + taps_w[tap][None, :] * lift_rows(masked, tap)
     d_conv_w = jnp.stack(d_conv_taps)
     d_pair = jnp.stack([d_x_branch, d_y_branch]).astype(jnp.bfloat16)
-    d_w_xy = jnp.einsum("td,ktc->kdc", n_one, d_pair, preferred_element_type=jnp.float32)
     d_n_one_part = jnp.einsum("ktc,kdc->td", d_pair, w_pair, preferred_element_type=jnp.float32)
     gain_one_own = lax.dynamic_slice_in_dim(gain_one_f, fsdp_pos * width_own, width_own, 0)
     rows_own = lax.dynamic_slice_in_dim(rows_f, fsdp_pos * width_own, width_own, 1)
@@ -284,22 +470,18 @@
     d_tokens = d_h_own + r_one * v_one - rows_own * r_one**3 * row_stat / width
     d_gain_one = jnp.sum(d_n_one * rows_own * r_one, axis=0)
     d_gain_two = lax.dynamic_slice_in_dim(d_gain_two_all, fsdp_pos * width_own, width_own, 0)
-    d_w_xy_four = d_w_xy.reshape(2, width, heads, block_own)
-    d_w_out_three = d_w_out.reshape(heads, block_own, width)
-    red_w_xy, red_gate_w, red_w_out = tuple(
-        (
-            part.astype(jnp.float32)
-            for part in sum_packed(
-                (
-                    d_w_xy_four.astype(jnp.bfloat16),
-                    d_gate_w.astype(jnp.bfloat16),
-                    d_w_out_three.astype(jnp.bfloat16),
-                ),
-                "rep",
-                (1, 2, 2),
-            )
-        )
-    )
+    turned = lambda v: v.T.reshape(4, 4, 160, 256)
+    red = grads(
+        turned(n_two), turned(d_top_low), turned(n_one), turned(d_rec), dg_t, du_t, hid_t, d_pair, mixed
+    )
+    cols = lambda v: jnp.moveaxis(v, 0, 1).reshape(80, -1)
+    red_w_in = jnp.stack([cols(red[0:3]), cols(red[3:6])])
+    red_w_down = cols(red[6:9]).T
+    red_w_xy = red[9:11].reshape(2, 80, heads, block_own)
+    red_w_out = red[11].T.reshape(heads, block_own, 80)
+    gate_lines = jnp.moveaxis(d_gate_w, 2, 0).reshape(256, -1).astype(jnp.bfloat16)
+    gate_own = lax.psum_scatter(gate_lines, "rep", scatter_dimension=0, tiled=True)
+    red_gate_w = jnp.moveaxis(gate_own.astype(jnp.float32).reshape(8, 2, heads, block_own), 0, 2)
     sum_g1, sum_g2, sum_conv_w, sum_conv_b, sum_gate_b, sum_decay = in_one(
         (
             d_gain_one,

time: 1740 us -> 750 us (0.43)
  waiting for transfers between devices: 1200 us -> 145 us
  Pallas kernels: 0 us -> 228 us
  local copies, waits for them, and re-layouts: 302 us -> 164 us
  matrix products: 82.6 us -> 16.5 us
  blocking collectives: 0 us -> 51.9 us
    unnamed x8 -> x4, waiting for transfers between devices: 537 us -> 0.07 us
    reduce_scatter x2 -> x1, waiting for transfers between devices: 454 us -> 0.01 us  [body(): lax.psum_scatter(gate_lines, 'rep', scatter_dimension=0, tiled=True)]
    pallas_call x0 -> x2, Pallas kernels: none -> 228 us  [the longest x1 202 us: grads(): pl.pallas_call(functools.partial(grads_kernel, g), out_shape=jax.ShapeDty...]
    convert_element_type x9 -> x2, local copies, waits for them, and re-layouts: 111 us -> 2.59 us  [the longest x1 2.53 us: body(): n_one = (rows_f * r_one * gain_one_f).astype(jnp.bfloat16)]
    dot_general x8 -> x0, matrix products: 65.5 us -> none  [the longest x1 11.6 us: body(): jnp.einsum('td,ktf->kdf', n_two, d_gate_up, preferred_element_type=jnp.fl...]
    all_to_all x3, waiting for transfers between devices: 85.8 us -> 31 us  [sum_at_owner(): lax.all_to_all(pieces, axis, split_axis=0, concat_axis=0, tiled=True)]
    reshape x4 -> x1, local copies, waits for them, and re-layouts: 53.1 us -> 0.86 us  [body(): cols = lambda v: jnp.moveaxis(v, 0, 1).reshape(80, -1)]
    psum x0 -> x1, blocking collectives: none -> 51.9 us  [body(): d_n_two = lax.psum(dn2_low.astype(jnp.float32), 'fsdp')]
  transfers between devices with their start and end apart: 14 -> 11, of which waited for: 12 -> 7; matrix products, arithmetic and copies ran while one was open for 18% -> 10% of each run, Pallas kernels for 0% -> 27%
where the time goes in v1:
time: 750 us; the launch traced here: 738 us
  Pallas kernels  228 us (30%)
  local copies, waits for them, and re-layouts  164 us (22%)
  waiting for transfers between devices  145 us (19%)
  other arithmetic  85.6 us (11%)
  blocking collectives  51.9 us (7%)
  starting transfers between devices  30.7 us (4%)
  matrix products  16.5 us (2%)
  between operations  15.8 us (2%)
    pallas_call x1, Pallas kernels, grads(): pl.pallas_call(functools.partial(grads_kernel, g), out_shape=jax.ShapeDty...  202 us
    slice x46, local copies, waits for them, and re-layouts, body(): states = lax.associative_scan(combine, (coeffs, inflow), axis=0)[1]  60.8 us
    all_to_all x4, waiting for transfers between devices, from_everyone(): lax.all_to_all(jnp.broadcast_to(value[None], (devices, *value.shape)), ax...  52.8 us
    psum x1, blocking collectives, body(): d_n_two = lax.psum(dn2_low.astype(jnp.float32), 'fsdp')  51.9 us
    reduce_scatter x1, waiting for transfers between devices, sum_in_two_steps(): own = lax.psum_scatter(padded, axis, scatter_dimension=0, tiled=True)  40.6 us
    all_to_all x3, waiting for transfers between devices, sum_at_owner(): lax.all_to_all(pieces, axis, split_axis=0, concat_axis=0, tiled=True)  31 us
    pallas_call x1, Pallas kernels, ffn(): pl.pallas_call(ffn_kernel, grid=(nt,), in_specs=[full, full, pl.BlockSpec...  26.5 us
    slice x52, local copies, waits for them, and re-layouts, body(): lax.associative_scan(combine, (jnp.flip(coeff_next, 0), jnp.flip(d_states...  26.5 us
  transfers between devices with their start and end apart: 11, of which 7 were waited for; matrix products, arithmetic and copies ran while one was open for 10% of the time, Pallas kernels for 27%

profile of v1, /device:TPU:0, one launch (start us, length us, event | category | flops | bytes accessed | tf_op | source)
XLA Modules:
  0.0 737.7 jit_solution(5845398651215648091)
XLA Ops:
  15.5 20.2 %all-gather.3.cloned.1.call-done = bf16[2560,258]{0,1:T(8,128)(2,1)} async-done(((bf16[640,258]{0,1:T(8,128)(2,1)}), bf16[2560,258]{0,1:T(8,128)(2,1)}) %all-gather.3.cloned.1.call-update) | async-done | bytes 1320976 | tf_op jit(solution)/shard_map/all_gather | solution.py:222
  38.9 5.2 convolution_bitcast_fusion.2
  51.1 4.3 all-to-all-start
  55.6 18.6 %all-to-all-done = bf16[4,256,10,64]{1,3,2,0:T(8,128)(2,1)} async-done(((bf16[4,256,10,64]{1,3,2,0:T(8,128)(2,1)}), bf16[4,256,10,64]{1,3,2,0:T(8,128)(2,1)}, u32[]{:S(2)}, u32[]{:S(2)}) %all-to-all-start) | async-done | bytes 1310752 | tf_op jit(solution)/shard_map/all_to_all | solution.py:234
  189.6 40.6 %reduce-scatter.5.cloned.1.call-done = f32[64,2560]{1,0:T(8,128)} async-done(((f32[256,2560]{1,0:T(8,128)}), f32[64,2560]{1,0:T(8,128)}) %reduce-scatter.5.cloned.1.call-update) | async-done | bytes 655376 | tf_op jit(solution)/shard_map/reduce_scatter | solution.py:258
  232.3 4.8 all-to-all-start.1
  237.7 29.0 %all-to-all-done.1 = bf16[4,256,640]{2,1,0:T(8,128)(2,1)} async-done(((bf16[4,256,640]{2,1,0:T(8,128)(2,1)}), bf16[4,256,640]{2,1,0:T(8,128)(2,1)}, u32[]{:S(2)}, u32[]{:S(2)}) %all-to-all-start.1) | async-done | bytes 1310752 | tf_op jit(solution)/shard_map/all_to_all | solution.py:234
  278.9 3.3 slice.618
  282.1 3.2 slice.627
  295.9 26.5 %ffn.1 = (bf16[3,256,640]{2,1,0:T(8,128)(2,1)}, bf16[3,256,640]{2,1,0:T(8,128)(2,1)}, bf16[3,256,640]{2,1,0:T(8,128)(2,1)}, bf16[256,2560]{1,0:T(8,128)(2,1)}, bf16[256,2560]{1,0:T(8,128)(2,1)}) custom-call(bf16[256,2560]{1,0:T(8,128)(2,1)} %get-tuple-element.189.n2, bf16[256,2560]{1,0:T(8,128)(2,1)} %get-tuple-element.190.dt, bf16[2,2560,1920]{2,1,0:T(8,128)(2,1)} %w_in.1, ...), custom_call_target="tpu_custom_call" | custom-call | tf_op jit(solution)/shard_map/ffn/pallas_call | solution.py:62
  322.4 51.9 %all-reduce.43 = f32[256,2560]{1,0:T(8,128)} all-reduce(bf16[256,2560]{1,0:T(8,128)(2,1)} %get-tuple-element.19), channel_id=1, replica_groups=mesh['rep'=32,'fsdp'=4] {'fsdp'}, use_global_device_ids=true, to_apply=%region_9.10 | all-reduce | flops 655360 | bytes 3932160 | tf_op jit(solution)/shard_map/psum | solution.py:418
  374.4 3.4 multiply_reduce_fusion
  378.4 3.8 convert_bitcast_fusion.1
  397.9 4.3 rev.6
  410.3 4.3 all-to-all-start.3
  418.0 15.5 %all-to-all-done.3 = bf16[4,256,10,64]{1,3,2,0:T(8,128)(2,1)} async-done(((bf16[4,256,10,64]{1,3,2,0:T(8,128)(2,1)}), bf16[4,256,10,64]{1,3,2,0:T(8,128)(2,1)}, u32[]{:S(2)}, u32[]{:S(2)}) %all-to-all-start.3) | async-done | bytes 1310752 | tf_op jit(solution)/shard_map/all_to_all | solution.py:271
  441.7 4.7 fusion
  447.7 4.3 all-to-all-start.4
  466.0 201.9 %grads.1 = f32[12,80,640]{2,1,0:T(8,128)} custom-call(bf16[4,4,160,256]{3,2,1,0:T(8,128)(2,1)} %bitcast.185, bf16[4,4,160,256]{3,2,1,0:T(8,128)(2,1)} %bitcast.186, bf16[4,4,160,256]{3,2,1,0:T(8,128)(2,1)} %bitcast.184, bf16[4,4,160,256]{3,2,1,0:T(8,128)(2,1)} %bitcast.187, bf16[3,256,640]{2,1,0:T(8,128)(2,1)} %get-tuple-element.20.dgs, ...), custom_call_target="tpu_custom_call" | custom-call | tf_op jit(solution)/shard_map/grads/pallas_call | solution.py:207
  671.5 5.0 all-to-all-start.2
  679.7 15.5 %all-to-all-done.2 = bf16[4,256,640]{2,1,0:T(8,128)(2,1)S(1)} async-done(((bf16[4,256,640]{2,1,0:T(8,128)(2,1)}), bf16[4,256,640]{2,1,0:T(8,128)(2,1)S(1)}, u32[]{:S(2)}, u32[]{:S(2)}) %all-to-all-start.2) | async-done | bytes 1310752 | tf_op jit(solution)/shard_map/all_to_all | solution.py:271
  695.8 3.2 all-to-all-start.5
  699.1 5.2 all-to-all-done.5
  705.7 4.6 all-to-all-start.6
  (466 shorter events, 238.4 us)
Async XLA Ops:
  7.2 178.9 %copy-start = (bf16[10,64,2560]{2,1,0:T(8,128)(2,1)S(1)}, bf16[10,64,2560]{2,1,0:T(8,128)(2,1)}, u32[]{:S(2)}) copy-start(bf16[10,64,2560]{2,1,0:T(8,128)(2,1)} %param.26) | copy-start | bytes 9830404
  7.2 28.5 %all-gather.3.cloned.1.call-start = ((), (), s32[]{:S(2)}) async-start(), calls=%async_computation.9 | async-start | bytes 1689600 | tf_op jit(solution)/shard_map/all_gather | solution.py:222
  13.0 68.9 %copy-start.64 = (pred[256]{0:T(512)(128)(4,1)}, pred[256]{0:T(512)(128)(4,1)S(1)}, u32[]{:S(2)}) copy-start(pred[256]{0:T(512)(128)(4,1)S(1)} %get-tuple-element.187) | copy-start | bytes 772
  14.3 30.1 %copy-start.46 = (f32[640]{0:T(1024)}, f32[640]{0:T(1024)S(1)}, u32[]{:S(2)}) copy-start(f32[640]{0:T(1024)S(1)} %mul.569) | copy-start | bytes 7684
  14.3 30.0 %copy-start.48 = (f32[640]{0:T(1024)}, f32[640]{0:T(1024)S(1)}, u32[]{:S(2)}) copy-start(f32[640]{0:T(1024)S(1)} %mul.564) | copy-start | bytes 7684
  14.4 30.0 %copy-start.50 = (f32[640]{0:T(1024)}, f32[640]{0:T(1024)S(1)}, u32[]{:S(2)}) copy-start(f32[640]{0:T(1024)S(1)} %mul.559) | copy-start | bytes 7684
  14.5 29.9 %copy-start.52 = (f32[640]{0:T(1024)}, f32[640]{0:T(1024)S(1)}, u32[]{:S(2)}) copy-start(f32[640]{0:T(1024)S(1)} %mul.551) | copy-start | bytes 7684
  15.5 28.9 %copy-start.58 = (f32[256]{0:T(256)}, f32[256]{0:T(256)S(1)}, u32[]{:S(2)}) copy-start(f32[256]{0:T(256)S(1)} %get-tuple-element.184) | copy-start | bytes 3076
  15.5 28.9 %copy-start.60 = (f32[256]{0:T(256)}, f32[256]{0:T(256)S(1)}, u32[]{:S(2)}) copy-start(f32[256]{0:T(256)S(1)} %get-tuple-element.185) | copy-start | bytes 3076
  15.5 28.9 %copy-start.62 = (f32[256]{0:T(256)}, f32[256]{0:T(256)S(1)}, u32[]{:S(2)}) copy-start(f32[256]{0:T(256)S(1)} %get-tuple-element.186) | copy-start | bytes 3076
  51.1 23.1 %all-to-all-start = ((bf16[4,256,10,64]{1,3,2,0:T(8,128)(2,1)}), bf16[4,256,10,64]{1,3,2,0:T(8,128)(2,1)}, u32[]{:S(2)}, u32[]{:S(2)}) async-start(bf16[4,256,10,64]{1,3,2,0:T(8,128)(2,1)} %broadcast_in_dim.51), calls=%async_computation | async-start | bytes 2621440 | tf_op jit(solution)/shard_map/all_to_all | solution.py:234
  55.4 174.7 %reduce-scatter.5.cloned.1.call-start = ((), (), s32[]{:S(2)}) async-start(), calls=%async_computation.10 | async-start | bytes 3276800 | tf_op jit(solution)/shard_map/reduce_scatter | solution.py:258
  55.6 26.3 %copy-start.68 = (f32[256]{0:T(256)}, f32[256]{0:T(256)S(1)}, u32[]{:S(2)}) copy-start(f32[256]{0:T(256)S(1)} %fusion.68) | copy-start | bytes 3076
  55.6 26.3 %copy-start.42 = (f32[640]{0:T(1024)}, f32[640]{0:T(1024)S(1)}, u32[]{:S(2)}) copy-start(f32[640]{0:T(1024)S(1)} %fusion.61) | copy-start | bytes 7684
  189.5 101.3 %all-gather.5.cloned.1.call-start = ((), (), s32[]{:S(2)}) async-start(), calls=%async_computation.11 | async-start | bytes 3276800 | tf_op jit(solution)/shard_map/all_gather | solution.py:259
  232.3 34.4 %all-to-all-start.1 = ((bf16[4,256,640]{2,1,0:T(8,128)(2,1)}), bf16[4,256,640]{2,1,0:T(8,128)(2,1)}, u32[]{:S(2)}, u32[]{:S(2)}) async-start(bf16[4,256,640]{2,1,0:T(8,128)(2,1)} %broadcast_in_dim.52), calls=%async_computation.2 | async-start | bytes 2621440 | tf_op jit(solution)/shard_map/all_to_all | solution.py:234
  410.3 23.1 %all-to-all-start.3 = ((bf16[4,256,10,64]{1,3,2,0:T(8,128)(2,1)}), bf16[4,256,10,64]{1,3,2,0:T(8,128)(2,1)}, u32[]{:S(2)}, u32[]{:S(2)}) async-start(bf16[4,256,10,64]{1,3,2,0:T(8,128)(2,1)} %bitcast.182), calls=%async_computation.4 | async-start | bytes 2621440 | tf_op jit(solution)/shard_map/all_to_all | solution.py:271
  447.7 223.8 %all-to-all-start.4 = ((bf16[4,256,640]{2,1,0:T(8,128)(2,1)}), bf16[4,256,640]{2,1,0:T(8,128)(2,1)}, u32[]{:S(2)}, u32[]{:S(2)}) async-start(bf16[4,256,640]{2,1,0:T(8,128)(2,1)} %bitcast.161), calls=%async_computation.5 | async-start | bytes 2621440 | tf_op jit(solution)/shard_map/all_to_all | solution.py:271
  452.0 269.7 %reduce-scatter.7.cloned.1.call-start = ((), (), s32[]{:S(2)}) async-start(), calls=%async_computation.12 | async-start | bytes 675840 | tf_op jit(solution)/shard_map/reduce_scatter | solution.py:483
  671.5 27.7 %copy-start.55 = (f32[640]{0:T(1024)S(1)}, f32[640]{0:T(1024)}, u32[]{:S(2)}) copy-start(f32[640]{0:T(1024)} %copy-done.54) | copy-start | bytes 7684
  671.5 23.8 %all-to-all-start.2 = ((bf16[4,256,640]{2,1,0:T(8,128)(2,1)}), bf16[4,256,640]{2,1,0:T(8,128)(2,1)S(1)}, u32[]{:S(2)}, u32[]{:S(2)}) async-start(bf16[4,256,640]{2,1,0:T(8,128)(2,1)} %bitcast.163), calls=%async_computation.3 | async-start | bytes 2621440 | tf_op jit(solution)/shard_map/all_to_all | solution.py:271
  678.1 21.0 %copy-start.17 = (f32[256,640]{1,0:T(8,128)}, f32[256,640]{1,0:T(8,128)S(1)}, u32[]{:S(2)}) copy-start(f32[256,640]{1,0:T(8,128)S(1)} %convert_reduce_fusion) | copy-start | bytes 1966084
  695.8 8.5 %all-to-all-start.5 = ((f32[4,256,1]{1,2,0:T(1,128)}), f32[4,256,1]{1,2,0:T(1,128)S(1)}, u32[]{:S(2)}, u32[]{:S(2)}) async-start(f32[4,256,1]{1,2,0:T(1,128)} %broadcast_in_dim.54), calls=%async_computation.6 | async-start | bytes 8192 | tf_op jit(solution)/shard_map/all_to_all | solution.py:234
  705.7 20.1 %all-to-all-start.6 = ((f32[32,1,6400]{2,1,0:T(1,128)}), f32[32,1,6400]{2,1,0:T(1,128)}, u32[]{:S(2)}, u32[]{:S(2)}) async-start(f32[32,1,6400]{2,1,0:T(1,128)} %broadcast_in_dim.55), calls=%async_computation.7 | async-start | bytes 1638400 | tf_op jit(solution)/shard_map/all_to_all | solution.py:234
  (59 other events, 250.2 us)
Sparse Core Ops, SparseCore 0:
  10.8 24.9 all-gather.2
  189.6 40.4 reduce-scatter.4
  231.9 39.4 all-gather.4
  465.1 213.4 reduce-scatter.6

commit v2 on v1

v2 whole, which is shorter than its diff:
```python
import functools

import jax
import jax.numpy as jnp
from jax import lax
from jax.experimental import pallas as pl
from jax.experimental.pallas import tpu as pltpu
from jax.sharding import PartitionSpec as P

MESH = pl.DeviceIdType.MESH
VM = 60 * 2**20
GC = 0.7978845608028654

def gelu_parts(v):
    v2 = v * v
    t = jnp.tanh(GC * v * (1.0 + 0.044715 * v2))
    half = 0.5 * (1.0 + t)
    g = v * half
    dg = half + 0.5 * v * (1.0 - t * t) * (GC * (1.0 + 3 * 0.044715 * v2))
    return g, dg

def dot(a, b):
    return jnp.dot(a, b, preferred_element_type=jnp.float32)

def dot_nt(a, b):
    return lax.dot_general(a, b, (((1,), (1,)), ((), ())), preferred_element_type=jnp.float32)

def ffn_kernel(n2, dt, w_in, w_dn, hid, dg, du, mlp, dn2, n2t, dtt, am, ad):
    i = pl.program_id(0)
    @pl.when(i == 1)
    def _():
        for c in range(4):
            n2t[c] = n2[:, c * 640:c * 640 + 640].T.reshape(4, 160, 256)
            dtt[c] = dt[:, c * 640:c * 640 + 640].T.reshape(4, 160, 256)
    @pl.when(i == 0)
    def _():
        am[...] = jnp.zeros_like(am)
        ad[...] = jnp.zeros_like(ad)
    gate = dot(n2[...], w_in[0])
    up = dot(n2[...], w_in[1])
    g, dgl = gelu_parts(gate)
    h = (g * up).astype(jnp.bfloat16)
    hid[0] = h
    dh = dot_nt(dt[...], w_dn[...])
    a = (dh * up * dgl).astype(jnp.bfloat16)
    b = (dh * g).astype(jnp.bfloat16)
    dg[0] = a
    du[0] = b
    am[...] += dot(h, w_dn[...])
    ad[...] += dot_nt(a, w_in[0])
    ad[...] += dot_nt(b, w_in[1])
    @pl.when(i == 2)
    def _():
        for c in range(4):
            mlp[c] = am[:, c * 640:c * 640 + 640].astype(jnp.bfloat16).reshape(4, 64, 640)
            dn2[c] = ad[:, c * 640:c * 640 + 640].astype(jnp.bfloat16).reshape(4, 64, 640)

def ffn(n2, dt, w_in, w_dn):
    R, D = n2.shape
    T = 640
    nt = w_dn.shape[0] // T
    full = pl.BlockSpec((R, D), lambda i: (0, 0))
    tile = pl.BlockSpec((1, R, T), lambda i: (i, 0, 0))
    ch = jax.ShapeDtypeStruct((nt, R, T), jnp.bfloat16)
    rd = jax.ShapeDtypeStruct((4, 4, 64, 640), jnp.bfloat16)
    td = jax.ShapeDtypeStruct((4, 4, 160, 256), jnp.bfloat16)
    part = pl.BlockSpec((4, 4, 64, 640), lambda i: (0, 0, 0, 0))
    turned = pl.BlockSpec((4, 4, 160, 256), lambda i: (0, 0, 0, 0))
    return pl.pallas_call(
        ffn_kernel, grid=(nt,),
        in_specs=[full, full, pl.BlockSpec((2, D, T), lambda i: (0, 0, i)), pl.BlockSpec((T, D), lambda i: (i, 0))],
        out_specs=[tile, tile, tile, part, part, turned, turned],
        out_shape=[ch, ch, ch, rd, rd, td, td],
        scratch_shapes=[pltpu.VMEM((R, D), jnp.float32)] * 2,
        compiler_params=pltpu.CompilerParams(vmem_limit_bytes=VM),
        name="ffn",
    )(n2, dt, w_in, w_dn)

def coords():
    r = lax.axis_index("rep")
    f = lax.axis_index("fsdp")
    return r // 8, (r // 2) % 4, r % 2, f

def peer(axis, d):
    x, z, y, f = coords()
    if axis == "x":
        x = (x + d) % 4
    elif axis == "z":
        z = (z + d) % 4
    elif axis == "y":
        y = 1 - y
    else:
        f = (f + d) % 4
    return ((x * 4 + z) * 2 + y, f)

class Grads:
    def __init__(self, plan, fplan):
        self.plan = plan
        self.fplan = fplan
    def scratch(self):
        n, m = len(self.plan), len(self.fplan)
        b = jnp.bfloat16
        return [
            pltpu.VMEM((n, 4, 256, 640), b),
            pltpu.VMEM((m, 4, 160, 1024), b),
            pltpu.VMEM((n, 4, 160, 640), b),
            pltpu.VMEM((n, 3, 160, 640), b),
            pltpu.VMEM((n, 2, 80, 640), b),
            pltpu.VMEM((n, 80, 640), b),
            pltpu.SemaphoreType.DMA((n, 3)), pltpu.SemaphoreType.DMA((n, 3)),
            pltpu.SemaphoreType.DMA((m, 3)), pltpu.SemaphoreType.DMA((m, 3)),
            pltpu.SemaphoreType.DMA((n, 3)), pltpu.SemaphoreType.DMA((n, 3)),
            pltpu.SemaphoreType.DMA((n,)), pltpu.SemaphoreType.DMA((n,)),
            pltpu.SemaphoreType.DMA((n,)), pltpu.SemaphoreType.DMA((m,)),
        ]
    def bind(self, refs, usrc, fsrc, out):
        (self.ub, self.ft, self.st, self.rr, self.tt, self.yr, self.us, self.ur, self.fs, self.fr,
         self.rq, self.rv, self.ys, self.yv, self.lu, self.lf) = refs
        self.usrc, self.fsrc, self.out = usrc, fsrc, out
    def rc(self, src, dst, s, r, axis, d):
        return pltpu.make_async_remote_copy(src_ref=src, dst_ref=dst, send_sem=s, recv_sem=r, device_id=peer(axis, d), device_id_type=MESH)
    def fcopies(self, k):
        i, axis = self.fplan[k]
        x, z, y, f = coords()
        src = self.fsrc[i]
        me = x if axis == "x" else z
        pick = (lambda t: src.at[t]) if axis == "x" else (lambda t: src.at[:, t])
        loc = pltpu.make_async_copy(pick(me), self.ft.at[k, :, :, pl.ds(0, 256)], self.lf.at[k])
        rem = [self.rc(pick((me + d) % 4), self.ft.at[k, :, :, pl.ds(d * 256, 256)], self.fs.at[k, d - 1], self.fr.at[k, d - 1], axis, d) for d in (1, 3, 2)]
        return loc, rem
    def ucopies(self, c):
        k, axis = self.plan[c]
        src = self.usrc(c)
        loc = pltpu.make_async_copy(src, self.ub.at[c, 0], self.lu.at[c])
        rem = [self.rc(src, self.ub.at[c, d], self.us.at[c, d - 1], self.ur.at[c, d - 1], axis, d) for d in (1, 3, 2)]
        return loc, rem
    def rscopies(self, c):
        k, axis = self.plan[c]
        ra = "z" if axis == "x" else "x"
        x, z, y, f = coords()
        me = z if axis == "x" else x
        return me, [self.rc(self.st.at[c, (me + d) % 4], self.rr.at[c, d - 1], self.rq.at[c, d - 1], self.rv.at[c, d - 1], ra, d) for d in (1, 3, 2)]
    def ycopy(self, c):
        x, z, y, f = coords()
        return self.rc(self.tt.at[c, 1 - y], self.yr.at[c], self.ys.at[c], self.yv.at[c], "y", 0)
    def send_f(self, k):
        loc, rem = self.fcopies(k)
        loc.start()
        for r in rem: r.start()
    def send_u(self, c):
        loc, rem = self.ucopies(c)
        loc.start()
        for r in rem: r.start()
    def mm(self, c):
        k, axis = self.plan[c]
        loc, rem = self.ucopies(c)
        loc.wait()
        for r in rem: r.wait()
        if not self.fdone[k]:
            loc, rem = self.fcopies(k)
            loc.wait()
            for r in rem: r.wait()
            self.fdone[k] = True
        self.st[c] = dot(self.ft[k].reshape(640, 1024), self.ub[c].reshape(1024, 640)).astype(jnp.bfloat16).reshape(4, 160, 640)
        me, cps = self.rscopies(c)
        for r in cps: r.start()
    def rs(self, c):
        me, cps = self.rscopies(c)
        for r in cps: r.wait()
        f = jnp.float32
        t = (self.st[c, me].astype(f) + self.rr[c, 0].astype(f)) + (self.rr[c, 1].astype(f) + self.rr[c, 2].astype(f))
        self.tt[c] = t.astype(jnp.bfloat16).reshape(2, 80, 640)
        self.ycopy(c).start()
    def fin(self, c):
        x, z, y, f = coords()
        self.ycopy(c).wait()
        self.out[c] = self.tt[c, y].astype(jnp.float32) + self.yr[c].astype(jnp.float32)

def entry_barrier(peers):
    b = pltpu.get_barrier_semaphore()
    for axis, d in peers:
        pl.semaphore_signal(b, inc=1, device_id=peer(axis, d), device_id_type=MESH)
    pl.semaphore_wait(b, len(peers))

REP = [("x", 1), ("x", 2), ("x", 3), ("z", 1), ("z", 2), ("z", 3), ("y", 1)]

PLAN = [(0, "x")] * 6 + [(1, "z")] * 3 + [(2, "x"), (3, "z"), (4, "z")]
FPLAN = [(0, "x"), (1, "z"), (2, "x"), (2, "z"), (3, "z")]

def grads_kernel(g, n2t, dtt, n1t, drt, dgs, dus, hids, dxs, zs, out, *refs):
    def usrc(c):
        if c < 3: return dgs.at[c]
        if c < 6: return dus.at[c - 3]
        if c < 9: return hids.at[c - 6]
        if c < 11: return dxs.at[c - 9]
        return zs
    g.bind(refs, usrc, [n2t, dtt, n1t, drt], out)
    g.fdone = [False] * len(g.fplan)
    entry_barrier(REP)
    g.send_f(0); g.send_f(1)
    order = [0, 6, 1, 3, 7, 2, 4, 8, 5, 9, 10, 11]
    for j, c in enumerate(order):
        if j == 6:
            for k in (2, 3, 4): g.send_f(k)
        g.send_u(c)
    n = len(order)
    for j in range(n + 4):
        if j < n: g.mm(order[j])
        if 0 <= j - 2 < n: g.rs(order[j - 2])
        if 0 <= j - 4 < n: g.fin(order[j - 4])

def grads(n2t, dtt, n1t, drt, dgs, dus, hids, dxs, zs):
    g = Grads(PLAN, FPLAN)
    return pl.pallas_call(
        functools.partial(grads_kernel, g),
        out_shape=jax.ShapeDtypeStruct((12, 80, 640), jnp.float32),
        in_specs=[pl.BlockSpec(memory_space=pl.ANY)] * 9,
        out_specs=pl.BlockSpec(memory_space=pltpu.VMEM),
        scratch_shapes=g.scratch(),
        compiler_params=pltpu.CompilerParams(collective_id=7, has_side_effects=True, vmem_limit_bytes=VM),
        name="grads",
    )(n2t, dtt, n1t, drt, dgs, dus, hids, dxs, zs)

F32 = jnp.float32
BF = jnp.bfloat16
EPS = 1e-06
ANY = pl.BlockSpec(memory_space=pl.ANY)
VMEM = pl.BlockSpec(memory_space=pltpu.VMEM)

def fpeer(d):
    r = lax.axis_index("rep")
    f = lax.axis_index("fsdp")
    h, c = f // 2, f % 2
    if d % 2:
        c = 1 - c
    if d // 2:
        h = 1 - h
    return r, h * 2 + c

class Comm:
    def __init__(self, ssem, rsem, lsem):
        self.ssem, self.rsem, self.lsem = ssem, rsem, lsem
        self.n = self.m = 0
        self.open = []
    def remote(self, src, dst, dev):
        k = self.n
        self.n += 1
        c = pltpu.make_async_remote_copy(src_ref=src, dst_ref=dst, send_sem=self.ssem.at[k], recv_sem=self.rsem.at[k], device_id=dev, device_id_type=MESH)
        c.start()
        self.open.append(c)
        return c
    def local(self, src, dst):
        k = self.m
        self.m += 1
        c = pltpu.make_async_copy(src, dst, self.lsem.at[k])
        c.start()
        return c
    def drain(self):
        for c in self.open:
            c.wait_send()
        self.open = []

class Gather:
    def __init__(self, comm, buf, own=None, parts=None):
        self.comm, self.buf = comm, buf
        self.f = lax.axis_index("fsdp")
        self.parts = parts or [()]
        self.own = own
        self.far, self.near = [], []
    def start(self):
        f, cm = self.f, self.comm
        for p in self.parts:
            dst = self.buf.at[(f, *p)]
            src = self.own.at[p] if self.own is not None else dst
            self.far.append(cm.remote(src, dst, fpeer(2)))
            self.near.append(cm.remote(src, dst, fpeer(1)))
    def relay(self):
        _, o = fpeer(2)
        self.late = []
        for p, c in zip(self.parts, self.far):
            c.wait_recv()
            dst = self.buf.at[(o, *p)]
            self.late.append(self.comm.remote(dst, dst, fpeer(1)))
    def finish(self):
        for c in self.near + self.late:
            c.wait_recv()

class Reduce:
    def __init__(self, comm, part, r1, s2, r2):
        self.comm, self.part, self.r1, self.s2, self.r2 = comm, part, r1, s2, r2
        self.f = lax.axis_index("fsdp")
        self.a, self.b, self.c = {}, {}, {}
    def send(self, c):
        _, o1 = fpeer(1)
        _, o3 = fpeer(3)
        self.a[c] = self.comm.remote(self.part.at[c, o3], self.r1.at[c, 1], fpeer(1))
        self.b[c] = self.comm.remote(self.part.at[c, o1], self.r1.at[c, 0], fpeer(1))
    def mid(self, c):
        _, o2 = fpeer(2)
        self.a[c].wait_recv()
        self.s2[c] = (self.part[c, o2].astype(F32) + self.r1[c, 1].astype(F32)).astype(BF)
        self.c[c] = self.comm.remote(self.s2.at[c], self.r2.at[c], fpeer(2))
    def fin(self, c):
        self.b[c].wait_recv()
        self.c[c].wait_recv()
        return self.part[c, self.f].astype(F32) + self.r1[c, 0].astype(F32) + self.r2[c].astype(F32)

def group_barrier(ds):
    b = pltpu.get_barrier_semaphore()
    for d in ds:
        pl.semaphore_signal(b, inc=1, device_id=fpeer(d), device_id_type=MESH)
    pl.semaphore_wait(b, len(ds))

def lanes(q):
    return slice(q * 128, q * 128 + 128)

def row_masks(lenc, ownc, ownr, msk):
    me = lax.axis_index("rep")
    ln = lenc[...]
    own = ownc[...] == me
    mine = jnp.where(own, ln, 0)
    j = lax.broadcasted_iota(jnp.int32, (128, 128), 0)
    i = lax.broadcasted_iota(jnp.int32, (128, 128), 1)
    offset = jnp.sum(jnp.where(j < i, mine, 0), axis=0, keepdims=True)
    total = jnp.sum(mine, axis=0, keepdims=True)
    place = lax.broadcasted_iota(jnp.int32, (256, 128), 0)
    hit = jnp.where((ownr[...] == me) & (offset == place), 1.0, 0.0)
    start = jnp.broadcast_to(jnp.max(hit, axis=1, keepdims=True), (256, 128))
    msk[0] = start
    run = start
    for k in (1, 2, 3):
        msk[k] = jnp.where((run == 0.0) & (place >= k), 1.0, 0.0)
        run = jnp.maximum(run, jnp.where(place >= k, pltpu.roll(start, k, axis=0), 0.0))
    msk[4] = jnp.where(place < total, 1.0, 0.0)

def wide_gates(gw, wg):
    row = lax.broadcasted_iota(jnp.int32, (128, 128), 0) // 64
    col = lax.broadcasted_iota(jnp.int32, (128, 128), 1) // 64
    for q in range(5):
        for k in range(2):
            for g in range(2):
                v = gw[k, q * 128:q * 128 + 128, g * 128:g * 128 + 128].astype(F32)
                r = pltpu.roll(v, 64, axis=1)
                for e in range(2):
                    twice = jnp.where(col == e, v, r)
                    p = 2 * g + e
                    wg[q, k * 128:k * 128 + 128, p * 128:p * 128 + 128] = jnp.where(row == col, twice, 0.0).astype(BF)

def softplus(v):
    return jnp.maximum(v, 0.0) + jnp.log(1.0 + jnp.exp(-jnp.abs(v)))

def sigmoid(v):
    return 1.0 / (1.0 + jnp.exp(-v))

def scan_rows(a_ref, u_ref, h_ref, back):
    rows = lax.broadcasted_iota(jnp.int32, (8, 640), 0)
    carry = jnp.zeros((1, 640), F32)
    order = range(31, -1, -1) if back else range(32)
    for i in order:
        a = a_ref[i * 8:i * 8 + 8, :]
        u = u_ref[i * 8:i * 8 + 8, :]
        for s in (1, 2, 4):
            if back:
                ok = rows < 8 - s
                a2 = jnp.where(ok, pltpu.roll(a, 8 - s, axis=0), 1.0)
                u2 = jnp.where(ok, pltpu.roll(u, 8 - s, axis=0), 0.0)
            else:
                ok = rows >= s
                a2 = jnp.where(ok, pltpu.roll(a, s, axis=0), 1.0)
                u2 = jnp.where(ok, pltpu.roll(u, s, axis=0), 0.0)
            u = u + a * u2
            a = a * a2
        h = u + a * carry
        h_ref[i * 8:i * 8 + 8, :] = h
        carry = h[0:1, :] if back else h[7:8, :]

def gate_values(q, pre, par, start):
    gx = sigmoid(pre[:, 0:128] + par[5:6, lanes(q)])
    ga = sigmoid(pre[:, 128:256] + par[6:7, lanes(q)])
    return gx, ga

def decay_of(q, ga, par, start):
    sp = softplus(par[7:8, lanes(q)])
    a = jnp.exp(-8.0 * ga * sp)
    spread = 1.0 - a * a
    mult = jnp.where(start == 1.0, 1.0, jnp.sqrt(jnp.maximum(spread, 0.01)))
    return sp, a, spread, mult

def forward_kernel(lenc, ownc, ownr, par, gn, tok, cot, w_t, gw_h, wo_h,
                   n1_o, cv_o, xb_o, yb_o, gx_o, ga_o, hs_o, z_o, n2_o, dt_o, h1_o, msk_o, r_o, g_o, wg_o, tk_o, n1t_o,
                   tkb, ctb, gnb, wv, gw, wo, wg, n1, dt, cvb, xb, yb, gx, ga, aa, uu, hs, z, msk, pt, r1, s2, r2, h1, n2b, rs1, rs2, n1t,
                   ssem, rsem, lsem):
    cm = Comm(ssem, rsem, lsem)
    f = lax.axis_index("fsdp")
    lw = [cm.local(w_t.at[0], wv.at[0]), cm.local(gw_h, gw), cm.local(w_t.at[1], wv.at[1]), cm.local(wo_h, wo)]
    lt = [cm.local(tok, tkb.at[f]), cm.local(gn, gnb.at[f]), cm.local(cot, ctb.at[f])]
    group_barrier((1, 2))
    halves = [(pl.ds(0, 128),), (pl.ds(128, 128),)]
    gtk = Gather(cm, tkb, tok, halves)
    ggn = Gather(cm, gnb, gn)
    gct = Gather(cm, ctb, cot)
    ggn.start()
    gtk.start()
    gct.start()
    row_masks(lenc, ownc, ownr, msk)
    lw[1].wait()
    wide_gates(gw, wg)
    outs = [cm.local(msk, msk_o), cm.local(wg, wg_o)]
    ggn.relay()
    gtk.relay()
    for c in lt:
        c.wait()
    ggn.finish()
    gtk.finish()
    @pl.loop(0, 16)
    def _(i):
        rows = pl.ds(pl.multiple_of(i * 16, 16), 16)
        xs = [tkb[p, rows, :].astype(F32) for p in range(4)]
        ss = sum(jnp.sum(x * x, axis=-1, keepdims=True) for x in xs)
        r = lax.rsqrt(ss * (1.0 / 2560) + EPS)
        rs1[rows, :] = jnp.broadcast_to(r, (16, 128))
        for p in range(4):
            n1[rows, p * 640:p * 640 + 640] = (xs[p] * r * gnb[p, 0:1, :]).astype(BF)
    outs += [cm.local(n1, n1_o), cm.local(gnb, g_o), cm.local(tkb, tk_o)]
    lw[0].wait()
    xb[...] = dot_nt(n1[...], wv[0])
    outs.append(cm.local(xb, xb_o))
    for q in range(5):
        x = xb[:, lanes(q)]
        acc = par[4:5, lanes(q)] + par[0:1, lanes(q)] * x
        for k in (1, 2, 3):
            acc = acc + par[k:k + 1, lanes(q)] * pltpu.roll(x, k, axis=0) * msk[k]
        cvb[f, :, lanes(q)] = acc.astype(BF)
    gcv = Gather(cm, cvb, None, halves)
    gcv.start()
    lw[2].wait()
    yb[...] = dot_nt(n1[...], wv[1])
    outs.append(cm.local(yb, yb_o))
    gct.relay()
    gcv.relay()
    for c in range(4):
        n1t[c] = n1[:, c * 640:c * 640 + 640].T.reshape(4, 160, 256)
    outs.append(cm.local(n1t, n1t_o))
    gcv.finish()
    outs.append(cm.local(cvb, cv_o))
    for q in range(5):
        lhs = jnp.concatenate([cvb[p, :, lanes(q)] for p in range(4)], axis=1)
        pre = dot_nt(lhs, wg[q])
        gxq, gaq = gate_values(q, pre, par, msk[0])
        sp, a, spread, mult = decay_of(q, gaq, par, msk[0])
        gx[:, lanes(q)] = gxq
        ga[:, lanes(q)] = gaq
        aa[:, lanes(q)] = jnp.where(msk[0] == 1.0, 0.0, a)
        uu[:, lanes(q)] = mult * gxq * cvb[f, :, lanes(q)].astype(F32)
    outs += [cm.local(gx, gx_o), cm.local(ga, ga_o)]
    scan_rows(aa, uu, hs, False)
    for q in range(5):
        yg, _ = gelu_parts(yb[:, lanes(q)])
        z[:, lanes(q)] = (hs[:, lanes(q)] * yg).astype(BF)
    outs += [cm.local(hs, hs_o), cm.local(z, z_o)]
    lw[3].wait()
    red = Reduce(cm, pt, r1, s2, r2)
    for c in range(4):
        pt[c] = dot(z[...], wo[:, c * 640:c * 640 + 640]).astype(BF).reshape(4, 64, 640)
        red.send(c)
        if c: red.mid(c - 1)
    red.mid(3)
    gct.finish()
    @pl.loop(0, 16)
    def _(i):
        rows = pl.ds(pl.multiple_of(i * 16, 16), 16)
        live = jnp.broadcast_to(msk[4, rows, 0:1], (16, 640))
        for p in range(4):
            dt[rows, p * 640:p * 640 + 640] = (ctb[p, rows, :].astype(F32) * live).astype(BF)
    outs.append(cm.local(dt, dt_o))
    own = pl.ds(pl.multiple_of(f * 64, 64), 64)
    ss = jnp.zeros((64, 1), F32)
    for c in range(4):
        h = tkb[c, own, :].astype(F32) + red.fin(c)
        h1[:, c * 640:c * 640 + 640] = h
        ss = ss + jnp.sum(h * h, axis=-1, keepdims=True)
    r = lax.rsqrt(ss * (1.0 / 2560) + EPS)
    rs2[...] = jnp.broadcast_to(r, (64, 128))
    for c in range(4):
        cs = slice(c * 640, c * 640 + 640)
        n2b[f, :, cs] = (h1[:, cs] * r * gnb[c, 1:2, :]).astype(BF)
    gn2 = Gather(cm, n2b, None, [(pl.ds(0, 32),), (pl.ds(32, 32),)])
    gn2.start()
    outs += [cm.local(h1, h1_o), cm.local(rs1, r_o.at[pl.ds(0, 256)]), cm.local(rs2, r_o.at[pl.ds(256, 64)])]
    gn2.relay()
    gn2.finish()
    outs.append(cm.local(n2b, n2_o))
    for c in outs:
        c.wait()
    cm.drain()

def forward(lenc, ownc, ownr, par, gn, tok, cot, w_t, gw_t, wo):
    s = jax.ShapeDtypeStruct
    R = 256
    fw = s((R, 640), F32)
    out_shape = [s((R, 2560), BF), s((4, R, 640), BF), fw, fw, fw, fw, fw, s((R, 640), BF), s((4, 64, 2560), BF), s((R, 2560), BF),
                 s((64, 2560), F32), s((5, R, 128), F32), s((320, 128), F32), s((4, 8, 640), F32), s((5, 256, 512), BF), s((4, R, 640), BF), s((4, 4, 160, 256), BF)]
    V = pltpu.VMEM
    f640 = V((R, 640), F32)
    scratch = [V((4, R, 640), BF), V((4, R, 640), BF), V((4, 8, 640), F32), V((2, 640, 2560), BF), V((2, 640, 256), BF), V((640, 2560), BF),
               V((5, 256, 512), BF), V((R, 2560), BF), V((R, 2560), BF), V((4, R, 640), BF), f640, f640, f640, f640, f640, f640, f640,
               V((R, 640), BF), V((5, R, 128), F32), V((4, 4, 64, 640), BF), V((4, 2, 64, 640), BF), V((4, 64, 640), BF), V((4, 64, 640), BF),
               V((64, 2560), F32), V((4, 64, 2560), BF), V((R, 128), F32), V((64, 128), F32), V((4, 4, 160, 256), BF),
               pltpu.SemaphoreType.DMA((48,)), pltpu.SemaphoreType.DMA((48,)), pltpu.SemaphoreType.DMA((32,))]
    return pl.pallas_call(
        forward_kernel, out_shape=out_shape,
        in_specs=[VMEM] * 5 + [ANY] * 5,
        out_specs=[ANY] * len(out_shape),
        scratch_shapes=scratch,
        compiler_params=pltpu.CompilerParams(collective_id=3, has_side_effects=True, vmem_limit_bytes=VM),
        name="forward",
    )(lenc, ownc, ownr, par, gn, tok, cot, w_t, gw_t, wo)

def prep(seq_len, seq_owner, gain_1, gain_2, w_xy, conv_w, conv_b, gate_w, gate_b, a_param, w_out):
    lenc = seq_len.reshape(128, 1)
    ownc = seq_owner.reshape(128, 1)
    ownr = seq_owner.reshape(1, 128)
    fl = lambda v: v.astype(F32).reshape(-1, 640)
    par = jnp.concatenate([fl(conv_w), fl(conv_b), fl(gate_b), fl(a_param)], axis=0)
    gn = jnp.pad(jnp.stack([gain_1, gain_2]).astype(F32), ((0, 6), (0, 0)))
    w_t = jnp.transpose(w_xy, (0, 2, 3, 1)).reshape(2, 640, 2560)
    gw_t = jnp.swapaxes(gate_w, 2, 3).reshape(2, 640, 256)
    return lenc, ownc, ownr, par, gn, w_t, gw_t, w_out.reshape(640, 2560)

def dot_tn(a, b):
    return lax.dot_general(a, b, (((0,), (0,)), ((), ())), preferred_element_type=jnp.float32)

class Swap:
    def __init__(self, comm, src, dst):
        f = lax.axis_index("fsdp")
        self.cps = []
        for d in (3, 2, 1):
            _, t = fpeer(d)
            self.cps.append(comm.remote(src.at[t], dst.at[f], fpeer(d)))
        self.own = comm.local(src.at[f], dst.at[f])
    def finish(self):
        self.own.wait()
        for c in self.cps:
            c.wait_recv()

def backward_kernel(par, mlp_h, dn2_h, cv_h, xb_h, yb_h, gx_h, ga_h, hs_h, msk_h, r_h, g_h, wg_h, tk_h, dt_h, h1_h, w_t, wo_h,
                    bo_o, dtok_o, dxy_o, dr_o, drt_o, sg_o, sm_o,
                    pm, pd, cv, xb, yb, gx, ga, hs, msk, rb, gnb, wg, tk, dtb, h1, wv, wo,
                    aa, uu, gg, dc1, dr, pb, dp, dxy, dna, dnp, dh1, bo, bob, dto, dtr, gs, gr, sm, sg, dob,
                    m1, m2, m3, d1, d2, d3, e1, e2, e3, f1, f2, f3,
                    ssem, rsem, lsem):
    cm = Comm(ssem, rsem, lsem)
    f = lax.axis_index("fsdp")
    own = pl.ds(pl.multiple_of(f * 64, 64), 64)
    ld = [cm.local(dn2_h.at[c], pd.at[c]) for c in range(4)]
    lh = [cm.local(h1_h, h1), cm.local(g_h, gnb), cm.local(r_h, rb), cm.local(dt_h.at[own], dtb), cm.local(msk_h, msk)]
    lm = [cm.local(mlp_h.at[c], pm.at[c]) for c in range(4)]
    lb = [cm.local(wo_h, wo), cm.local(yb_h, yb), cm.local(hs_h, hs), cm.local(ga_h, ga), cm.local(gx_h, gx), cm.local(cv_h, cv),
          cm.local(wg_h, wg), cm.local(xb_h, xb), cm.local(w_t, wv), cm.local(tk_h.at[:, own], tk)]
    group_barrier((1, 2, 3))
    rd = Reduce(cm, pd, d1, d2, d3)
    rm = Reduce(cm, pm, m1, m2, m3)
    for c in range(4):
        ld[c].wait()
        rd.send(c)
    for c in range(4):
        rd.mid(c)
    for c in range(4):
        lm[c].wait()
        rm.send(c)
    for c in lh:
        c.wait()
    gs[...] = jnp.zeros_like(gs)
    r2 = rb[256:320, 0:1]
    acc = jnp.zeros((64, 1), F32)
    for c in range(4):
        cs = slice(c * 640, c * 640 + 640)
        dn = rd.fin(c)
        h = h1[:, cs]
        gs[c, 1:2, :] = jnp.sum(dn * h * r2, axis=0, keepdims=True)
        v = dn * gnb[c, 1:2, :]
        dh1[:, cs] = v
        acc = acc + jnp.sum(v * h, axis=-1, keepdims=True)
    acc = acc * (1.0 / 2560) * (r2 * r2 * r2)
    for c in range(4):
        cs = slice(c * 640, c * 640 + 640)
        d = dtb[:, cs].astype(F32) + r2 * dh1[:, cs] - h1[:, cs] * acc
        dh1[:, cs] = d
        dr[f, :, cs] = d.astype(BF)
    gdr = Gather(cm, dr, None, [(pl.ds(0, 32),), (pl.ds(32, 32),)])
    gdr.start()
    for c in range(4):
        rm.mid(c)
    for c in lb:
        c.wait()
    gdr.relay()
    for q in range(5):
        sp, a, spread, mult = decay_of(q, ga[:, lanes(q)], par, msk[0])
        up = pltpu.roll(jnp.where(msk[0] == 1.0, 0.0, a), 255, axis=0)
        rows = lax.broadcasted_iota(jnp.int32, (256, 128), 0)
        aa[:, lanes(q)] = jnp.where(rows == 255, 0.0, up)
    gdr.finish()
    uu[...] = dot_nt(dr[...].reshape(256, 2560), wo[...])
    outs = [cm.local(dr, dr_o)]
    for q in range(5):
        yg, dgl = gelu_parts(yb[:, lanes(q)])
        dz = uu[:, lanes(q)]
        dxy[1, :, lanes(q)] = (dz * hs[:, lanes(q)] * dgl).astype(BF)
        uu[:, lanes(q)] = dz * yg
    scan_rows(aa, uu, gg, True)
    re = Reduce(cm, pb, e1, e2, e3)
    for q in range(5):
        ls = lanes(q)
        start = msk[0]
        gxq, gaq, g = gx[:, ls], ga[:, ls], gg[:, ls]
        sp, a, spread, mult = decay_of(q, gaq, par, start)
        cvq = cv[f, :, ls].astype(F32)
        prev = jnp.where(start == 1.0, 0.0, pltpu.roll(hs[:, ls], 1, axis=0))
        slope = jnp.where((start == 1.0) | (spread <= 0.01), 0.0, -a / mult)
        da = g * prev + g * gxq * cvq * slope
        dc1[:, ls] = g * mult * gxq
        dlog = da * a
        da_p = jnp.sum(dlog * (-8.0 * gaq), axis=0, keepdims=True) * sigmoid(par[7:8, ls])
        px = (g * mult * cvq * gxq * (1.0 - gxq)).astype(BF)
        pa = (-8.0 * dlog * sp * gaq * (1.0 - gaq)).astype(BF)
        dp[q, :, 0:128] = px
        dp[q, :, 128:256] = pa
        sm[7:8, ls] = jnp.sum(px.astype(F32), axis=0, keepdims=True)
        sm[8:9, ls] = jnp.sum(pa.astype(F32), axis=0, keepdims=True)
        sm[9:10, ls] = da_p
        db = dot(dp[q], wg[q]).astype(BF)
        for p in range(4):
            pb[q, p] = db[:, lanes(p)]
        re.send(q)
        if q: re.mid(q - 1)
    re.mid(4)
    for c in range(4):
        cs = slice(c * 640, c * 640 + 640)
        dna[c] = dot(dxy[1], wv[1, :, cs])
    low = lax.broadcasted_iota(jnp.int32, (64, 128), 1) < 64
    for q in range(5):
        lhs = jnp.concatenate([cv[p, :, lanes(q)] for p in range(4)], axis=1)
        gwt = dot_tn(lhs, dp[q])
        for p in range(4):
            for k in range(2):
                blk = gwt[p * 128:p * 128 + 128, k * 128:k * 128 + 128]
                sg[k, q, p] = jnp.where(low, blk[0:64], blk[64:128]).astype(BF)
    outs.append(cm.local(sg, sg_o))
    live = msk[4, own, 0:1]
    for c in range(4):
        bo[c] = (live * (h1[:, c * 640:c * 640 + 640] + rm.fin(c))).astype(BF)
    sbo = Swap(cm, bo, bob)
    for q in range(5):
        ls = lanes(q)
        d = dc1[:, ls] + re.fin(q)
        x = xb[:, ls]
        sm[6:7, ls] = jnp.sum(d, axis=0, keepdims=True)
        sm[2:3, ls] = jnp.sum(d * x, axis=0, keepdims=True)
        dx = par[0:1, ls] * d
        for k in (1, 2, 3):
            m = d * msk[k]
            sm[2 + k:3 + k, ls] = jnp.sum(m * pltpu.roll(x, k, axis=0), axis=0, keepdims=True)
            dx = dx + par[k:k + 1, ls] * pltpu.roll(m, 256 - k, axis=0)
        dxy[0, :, ls] = dx.astype(BF)
    outs.append(cm.local(dxy, dxy_o))
    rf = Reduce(cm, dnp, f1, f2, f3)
    for c in range(4):
        cs = slice(c * 640, c * 640 + 640)
        dnp[c] = (dna[c] + dot(dxy[0], wv[0, :, cs])).astype(BF).reshape(4, 64, 640)
        rf.send(c)
        if c: rf.mid(c - 1)
    rf.mid(3)
    for p in range(4):
        for o in range(4):
            pass
    drt = dr[...].reshape(256, 2560)
    for c in range(4):
        dtr[c] = drt[:, c * 640:c * 640 + 640].T.reshape(4, 160, 256)
    outs.append(cm.local(dtr, drt_o))
    r1 = rb[own, 0:1]
    acc = jnp.zeros((64, 1), F32)
    for c in range(4):
        dn = rf.fin(c)
        x = tk[c].astype(F32)
        gs[c, 0:1, :] = jnp.sum(dn * x * r1, axis=0, keepdims=True)
        v = dn * gnb[c, 0:1, :]
        dna[c, 0:64, :] = v
        acc = acc + jnp.sum(v * x, axis=-1, keepdims=True)
    acc = acc * (1.0 / 2560) * (r1 * r1 * r1)
    for c in range(4):
        dob[c] = (dh1[:, c * 640:c * 640 + 640] + r1 * dna[c, 0:64, :] - tk[c].astype(F32) * acc).astype(BF)
    sdt = Swap(cm, dob, dto)
    gcp = []
    for d in (3, 2, 1):
        _, t = fpeer(d)
        gcp.append(cm.remote(gs.at[t], gr.at[d - 1], fpeer(d)))
    sbo.finish()
    outs.append(cm.local(bob, bo_o))
    for c in gcp:
        c.wait_recv()
    sm[0:2, :] = (gs[f, 0:2, :] + gr[0, 0:2, :]) + (gr[1, 0:2, :] + gr[2, 0:2, :])
    sm[10:16, :] = jnp.zeros((6, 640), F32)
    outs.append(cm.local(sm, sm_o))
    sdt.finish()
    uu[...] = dto[...].astype(F32).reshape(256, 640)
    outs.append(cm.local(uu, dtok_o))
    for c in outs:
        c.wait()
    cm.drain()

def backward(par, mlp, dn2, cv, xb, yb, gx, ga, hs, msk, r, g, wg, tk, dt, h1, w_t, wo):
    s = jax.ShapeDtypeStruct
    R = 256
    V = pltpu.VMEM
    out_shape = [s((4, 64, 640), BF), s((R, 640), F32), s((2, R, 640), BF), s((4, 64, 2560), BF), s((4, 4, 160, 256), BF), s((2, 5, 4, 64, 128), BF), s((16, 640), F32)]
    w = V((R, 640), F32)
    blk = V((4, 4, 64, 640), BF)
    red = [V((4, 2, 64, 640), BF), V((4, 64, 640), BF), V((4, 64, 640), BF)]
    red5 = [V((5, 2, R, 128), BF), V((5, R, 128), BF), V((5, R, 128), BF)]
    scratch = [blk, blk, V((4, R, 640), BF), w, w, w, w, w, V((5, R, 128), F32), V((320, 128), F32), V((4, 8, 640), F32), V((5, 256, 512), BF),
               V((4, 64, 640), BF), V((64, 2560), BF), V((64, 2560), F32), V((2, 640, 2560), BF), V((640, 2560), BF),
               w, w, w, w, V((4, 64, 2560), BF), V((5, 4, R, 128), BF), V((5, R, 256), BF), V((2, R, 640), BF), V((4, R, 640), F32), blk, V((64, 2560), F32),
               V((4, 64, 640), BF), V((4, 64, 640), BF), V((4, 64, 640), BF), V((4, 4, 160, 256), BF), V((4, 8, 640), F32), V((3, 8, 640), F32), V((16, 640), F32),
               V((2, 5, 4, 64, 128), BF), V((4, 64, 640), BF)] + red + red + red5 + red + [
               pltpu.SemaphoreType.DMA((80,)), pltpu.SemaphoreType.DMA((80,)), pltpu.SemaphoreType.DMA((40,))]
    return pl.pallas_call(
        backward_kernel, out_shape=out_shape,
        in_specs=[VMEM] + [ANY] * 17,
        out_specs=[ANY] * len(out_shape),
        scratch_shapes=scratch,
        compiler_params=pltpu.CompilerParams(collective_id=4, has_side_effects=True, vmem_limit_bytes=VM),
        name="backward",
    )(par, mlp, dn2, cv, xb, yb, gx, ga, hs, msk, r, g, wg, tk, dt, h1, w_t, wo)

def exchange(g, send, slots, ss, rs, axis):
    cps = [g.rc(send(d), slots.at[d - 1], ss.at[d - 1], rs.at[d - 1], axis, d) for d in (1, 3, 2)]
    for c in cps: c.start()
    return cps

def grads3_kernel(g, n2t, dtt, n1t, drt, dgs, dus, hids, dxy, zs, sg_h, sm_h, in_o, dn_o, xy_o, wout_o, gate_o, sm_o, red, sg, sgr, sgt, sgr2, sgy, sma, smr, smy, sems, semr, seml, *refs):
    def usrc(c):
        if c < 3: return dgs.at[c]
        if c < 6: return dus.at[c - 3]
        if c < 9: return hids.at[c - 6]
        if c < 11: return dxy.at[c - 9]
        return zs
    g.bind(refs, usrc, [n2t, dtt, n1t, drt], red)
    g.fdone = [False] * len(g.fplan)
    x, z, y, f = coords()
    lsg = pltpu.make_async_copy(sg_h, sg, seml.at[0]); lsg.start()
    lsm = pltpu.make_async_copy(sm_h, sma.at[0], seml.at[1]); lsm.start()
    entry_barrier(REP)
    lsm.wait()
    e1 = exchange(g, lambda d: sma.at[0], smr.at[0], sems.at[0], semr.at[0], "x")
    lsg.wait()
    e2 = exchange(g, lambda d: sg.at[(x + d) % 4], sgr, sems.at[1], semr.at[1], "x")
    g.send_f(0); g.send_f(1)
    order = [0, 6, 1, 3, 7, 2, 4, 8, 5, 9, 10, 11]
    for j, c in enumerate(order):
        if j == 6:
            for k in (2, 3, 4): g.send_f(k)
        g.send_u(c)
    n = len(order)
    for j in range(n + 4):
        if j < n: g.mm(order[j])
        if 0 <= j - 2 < n: g.rs(order[j - 2])
        if 0 <= j - 4 < n: g.fin(order[j - 4])
        if j == 0:
            for c in e1: c.wait()
            sma[1] = (sma[0] + smr[0, 0]) + (smr[0, 1] + smr[0, 2])
            e3 = exchange(g, lambda d: sma.at[1], smr.at[1], sems.at[2], semr.at[2], "z")
            for c in e2: c.wait()
            t = (sg[x].astype(F32) + sgr[0].astype(F32)) + (sgr[1].astype(F32) + sgr[2].astype(F32))
            sgt[...] = t.astype(BF)
            e4 = exchange(g, lambda d: sgt.at[:, :, pl.ds(pl.multiple_of((z + d) % 4 * 16, 16), 16)], sgr2, sems.at[3], semr.at[3], "z")
        if j == 2:
            for c in e3: c.wait()
            sma[2] = (sma[1] + smr[1, 0]) + (smr[1, 1] + smr[1, 2])
            e5 = g.rc(sma.at[2], smy, sems.at[4, 0], semr.at[4, 0], "y", 0); e5.start()
            for c in e4: c.wait()
            t = sgt[:, :, pl.ds(pl.multiple_of(z * 16, 16), 16), :].astype(F32) + sgr2[0].astype(F32) + sgr2[1].astype(F32) + sgr2[2].astype(F32)
            sgy[0] = t
            e6 = g.rc(sgy.at[0], sgy.at[1], sems.at[4, 1], semr.at[4, 1], "y", 0); e6.start()
        if j == 4:
            e5.wait()
            sm_o[...] = sma[2] + smy[...]
            e6.wait()
            half = pl.ds(pl.multiple_of(y * 8, 8), 8)
            gate_o[...] = sgy[0, :, :, half, :] + sgy[1, :, :, half, :]
    for k in range(2):
        for i in range(3):
            in_o[k, :, i * 640:i * 640 + 640] = red[3 * k + i]
        xy_o[k] = red[9 + k].T
    for i in range(3):
        dn_o[:, i * 640:i * 640 + 640] = red[6 + i]
    wout_o[...] = red[11].T

def grads3(n2t, dtt, n1t, drt, dgs, dus, hids, dxy, zs, sg, sm):
    g = Grads(PLAN, FPLAN)
    s = jax.ShapeDtypeStruct
    V = pltpu.VMEM
    return pl.pallas_call(
        functools.partial(grads3_kernel, g),
        out_shape=[s((2, 80, 1920), F32), s((80, 1920), F32), s((2, 640, 80), F32), s((640, 80), F32), s((2, 5, 8, 128), F32), s((16, 640), F32)],
        in_specs=[ANY] * 11,
        out_specs=[VMEM] * 6,
        scratch_shapes=[V((12, 80, 640), F32), V((4, 2, 5, 64, 128), BF), V((3, 2, 5, 64, 128), BF), V((2, 5, 64, 128), BF), V((3, 2, 5, 16, 128), BF), V((2, 2, 5, 16, 128), F32),
                        V((3, 16, 640), F32), V((2, 3, 16, 640), F32), V((16, 640), F32),
                        pltpu.SemaphoreType.DMA((5, 3)), pltpu.SemaphoreType.DMA((5, 3)), pltpu.SemaphoreType.DMA((2,))] + g.scratch(),
        compiler_params=pltpu.CompilerParams(collective_id=7, has_side_effects=True, vmem_limit_bytes=VM),
        name="grads",
    )(n2t, dtt, n1t, drt, dgs, dus, hids, dxy, zs, sg, sm)

def body(tokens, seq_len, seq_owner, gain_1, gain_2, w_xy, conv_w, conv_b, gate_w, gate_b, a_param, w_out, w_in, w_down, cotangent):
    lenc, ownc, ownr, par, gn, w_t, gw_t, wo = prep(seq_len, seq_owner, gain_1, gain_2, w_xy, conv_w, conv_b, gate_w, gate_b, a_param, w_out)
    (n1, cv, xb, yb, gx, ga, hs, z, n2, dt, h1, msk, r, g, wg, tk, n1t) = forward(lenc, ownc, ownr, par, gn, tokens, cotangent, w_t, gw_t, wo)
    hid, dg, du, mlp, dn2, n2t, dtt = ffn(n2.reshape(256, 2560), dt, w_in, w_down)
    bo, dtok, dxy, dr, drt, sg, sm = backward(par, mlp, dn2, cv, xb, yb, gx, ga, hs, msk, r, g, wg, tk, dt, h1, w_t, wo)
    r_in, r_dn, r_xy, r_wo, r_gate, r_sm = grads3(n2t, dtt, n1t, drt, dg, du, hid, dxy, z, jnp.moveaxis(sg, 2, 0), sm)
    red_xy = jnp.transpose(r_xy.reshape(2, 10, 64, 80), (0, 3, 1, 2))
    red_gate = jnp.transpose(r_gate.reshape(2, 5, 8, 2, 64), (0, 1, 3, 2, 4)).reshape(2, 10, 8, 64)
    return (bo.reshape(256, 640), dtok, r_sm[0], r_sm[1], red_xy, r_sm[2:6].reshape(4, 10, 64), r_sm[6].reshape(10, 64),
            red_gate, r_sm[7:9].reshape(2, 10, 64), r_sm[9].reshape(10, 64), r_wo.reshape(10, 64, 80), r_in, r_dn.T)


def solution(mesh):
    return jax.shard_map(
        body,
        mesh=mesh,
        in_specs=(
            P("rep", "fsdp"), P(), P(), P("fsdp"), P("fsdp"), P(None, None, None, "fsdp"), P(None, None, "fsdp"), P(None, "fsdp"),
            P(None, None, None, "fsdp"), P(None, None, "fsdp"), P(None, "fsdp"), P(None, "fsdp", None), P(None, None, "fsdp"), P("fsdp", None), P("rep", "fsdp"),
        ),
        out_specs=(
            P("rep", "fsdp"), P("rep", "fsdp"), P("fsdp"), P("fsdp"), P(None, "rep", None, "fsdp"), P(None, None, "fsdp"), P(None, "fsdp"),
            P(None, None, "rep", "fsdp"), P(None, None, "fsdp"), P(None, "fsdp"), P(None, "fsdp", "rep"), P(None, "rep", "fsdp"), P("fsdp", "rep"),
        ),
        check_vma=False,
    )
```

time: 750 us -> 379 us (0.51)
  waiting for transfers between devices: 145 us -> 0 us
  local copies, waits for them, and re-layouts: 164 us -> 21.4 us
  Pallas kernels: 228 us -> 348 us
  other arithmetic: 85.6 us -> 1.89 us
  blocking collectives: 51.9 us -> 0 us
  starting transfers between devices: 30.7 us -> 0 us
  matrix products: 16.5 us -> 0 us
  between operations: 15.8 us -> 0.98 us
    pallas_call x1 -> x3, Pallas kernels: 202 us -> 319 us  [the longest x1 203 us: grads3(): pl.pallas_call(functools.partial(grads3_kernel, g), out_shape=[s((2, 80,...]
    slice x113 -> x4, local copies, waits for them, and re-layouts: 89.4 us -> 4.01 us  [the longest x1 1.47 us: body(): r_sm[9].reshape(10, 64)]
    all_to_all x7 -> x0, waiting for transfers between devices: 83.8 us -> none  [the longest x4 52.8 us: from_everyone(): lax.all_to_all(jnp.broadcast_to(value[None], (devices, *value.shape)), ax...]
    psum x1 -> x0, blocking collectives: 51.9 us -> none  [body(): d_n_two = lax.psum(dn2_low.astype(jnp.float32), 'fsdp')]
    reduce_scatter x2 -> x0, waiting for transfers between devices: 40.6 us -> none  [the longest x1 40.6 us: sum_in_two_steps(): own = lax.psum_scatter(padded, axis, scatter_dimension=0, tiled=True)]
    all_to_all x7 -> x0, starting transfers between devices: 30.6 us -> none  [the longest x4 16.9 us: from_everyone(): lax.all_to_all(jnp.broadcast_to(value[None], (devices, *value.shape)), ax...]
    reduce_sum x15 -> x0, other arithmetic: 23.2 us -> none  [the longest x3 4.15 us: sum_at_owner(): return arrived.astype(jnp.float32).sum(axis=0)]
    all_gather x2 -> x0, waiting for transfers between devices: 20.2 us -> none  [the longest x1 20.2 us: gather_turned(): filled = lax.all_gather(both, axis, axis=0, tiled=True)]
  transfers between devices with their start and end apart: 11 -> 0, of which waited for: 7 -> 0; matrix products, arithmetic and copies ran while one was open for 10% -> 0% of each run, Pallas kernels for 27% -> 0%
where the time goes in v2:
time: 379 us; the launch traced here: 372 us
  Pallas kernels  348 us (92%)
  local copies, waits for them, and re-layouts  21.4 us (6%)
    pallas_call x1, Pallas kernels, grads3(): pl.pallas_call(functools.partial(grads3_kernel, g), out_shape=[s((2, 80,...  203 us
    pallas_call x1, Pallas kernels, backward(): pl.pallas_call(backward_kernel, out_shape=out_shape, in_specs=[VMEM] + [A...  61 us
    pallas_call x1, Pallas kernels, forward(): pl.pallas_call(forward_kernel, out_shape=out_shape, in_specs=[VMEM] * 5 +...  55 us
    pallas_call x1, Pallas kernels, ffn(): pl.pallas_call(ffn_kernel, grid=(nt,), in_specs=[full, full, pl.BlockSpec...  28.8 us

profile of v2, /device:TPU:0, one launch (start us, length us, event | category | flops | bytes accessed | tf_op | source)
XLA Modules:
  0.0 372.4 jit_solution(5737195629335538541)
XLA Ops:
  0.6 0.7 stack.9
  1.3 0.7 stack.10
  2.0 0.8 reshape.110
  2.8 0.8 reshape.93
  4.2 0.7 copy.36
  4.9 0.7 copy.35
  6.4 1.4 copy.37.lenc
  7.7 1.4 copy.38.ownc
  9.1 55.0 %forward.1 = (bf16[256,2560]{1,0:T(8,128)(2,1)}, bf16[4,256,640]{2,1,0:T(8,128)(2,1)}, f32[256,640]{1,0:T(8,128)}, f32[256,640]{1,0:T(8,128)}, f32[256,640]{1,0:...) custom-call(s32[128,1]{1,0:T(8,128)} %copy.37.lenc, ...), custom_call_target="tpu_custom_call" | custom-call | tf_op jit(solution)/shard_map/forward/pallas_call | solution.py:510
  64.2 28.8 %ffn.1 = (bf16[3,256,640]{2,1,0:T(8,128)(2,1)}, bf16[3,256,640]{2,1,0:T(8,128)(2,1)}, bf16[3,256,640]{2,1,0:T(8,128)(2,1)}, bf16[4,4,64,640]{3,2,1,0:T(8,128)(2,...) custom-call(bf16[256,2560]{1,0:T(8,128)(2,1)} %bitcast.26, ...), custom_call_target="tpu_custom_call" | custom-call | tf_op jit(solution)/shard_map/ffn/pallas_call | solution.py:69
  93.0 61.0 %backward.1 = (bf16[4,64,640]{2,1,0:T(8,128)(2,1)}, f32[256,640]{1,0:T(8,128)}, bf16[2,256,640]{2,1,0:T(8,128)(2,1)}, bf16[4,64,2560]{2,1,0:T(8,128)(2,1)}, bf16...) custom-call(f32[8,640]{1,0:T(8,128)} %pad_maximum_fusion.1.par, ...), custom_call_target="tpu_custom_call" | custom-call | tf_op jit(solution)/shard_map/backward/pallas_call | solution.py:726
  154.0 2.0 copy.43
  156.0 203.3 %grads.1 = (f32[2,80,1920]{2,1,0:T(8,128)}, f32[80,1920]{1,0:T(8,128)}, f32[2,640,80]{2,1,0:T(8,128)}, f32[640,80]{1,0:T(8,128)}, f32[2,5,8,128]{3,2,1,0:T(8,128)}, /*index=5*/f32[16,640]{1,0:T(8,128)}) custom-call(bf16[4,4,160,256]{3,2,1,0:T(8,128)(2,1)} %get-tuple-element.66.n2t, bf16[4,4,160,256]{3,2,1,0:T(8,128)(2,1)} %get-tuple-element.67.dtt, ...), custom_call_target="tpu_custom_call" | custom-call | tf_op jit(solution)/shard_map/grads/pallas_call | solution.py:802
  359.3 0.9 slice.30
  360.2 0.7 slice.26
  360.9 1.5 slice_reduce_fusion
  363.0 0.7 reshape_squeeze.6
  365.1 0.9 fusion.4
  366.7 0.7 copy.50
  367.4 0.8 copy.51
  368.2 0.8 copy.52
  369.1 0.7 copy.53
  369.8 1.0 copy.54
  371.3 0.8 copy.55
  (22 shorter events, 4.6 us)
Async XLA Ops:
  156.0 210.7 %copy-start.4 = (bf16[4,64,640]{2,1,0:T(8,128)(2,1)S(1)}, bf16[4,64,640]{2,1,0:T(8,128)(2,1)}, u32[]{:S(2)}) copy-start(bf16[4,64,640]{2,1,0:T(8,128)(2,1)} %get-tuple-element.64) | copy-start | bytes 983044
  359.3 8.1 %copy-start.1 = (f32[256,640]{1,0:T(8,128)S(1)}, f32[256,640]{1,0:T(8,128)}, u32[]{:S(2)}) copy-start(f32[256,640]{1,0:T(8,128)} %get-tuple-element.129) | copy-start | bytes 1966084
  359.3 9.0 %copy-start.2 = (f32[2,640,80]{2,1,0:T(8,128)S(1)}, f32[2,640,80]{2,1,0:T(8,128)}, u32[]{:S(2)}) copy-start(f32[2,640,80]{2,1,0:T(8,128)} %get-tuple-element.78) | copy-start | bytes 1228804
  367.4 1.7 copy-start.5
  368.2 1.6 copy-start
  369.8 1.5 copy-start.3
